TPU v7x, 32 devices: a whole 2x2x4 slice. The times are simulated.
32 devices in a mesh: seq: 16 (over z, y, x), head: 2 (over core).
Axes of the slice: x: 2, y: 2, z: 4, core: 2. Of those that a mesh axis runs over, the one named last changes fastest.
Arguments:
- queries: bfloat16 [4096, 4096], P('seq', 'head'), may hold values from -6 to 6
- key_rows: bfloat16 [4096, 4096], P('seq', 'head'), may hold values from -6 to 6
- value_rows: bfloat16 [4096, 4096], P('seq', 'head'), may hold values from -6 to 6
- doc_block: int32 [32], P('seq'), may hold values from 0 to 4, never falling along the last dimension, each value on 1 to 16 neighbouring positions
- out_weight: bfloat16 [4096, 4096], P('head'), may hold values from -0.09375 to 0.09375
- grad_output: bfloat16 [4096, 4096], P('seq'), may hold values from -8 to 8
Outputs:
- projected: bfloat16 [4096, 4096], P('seq', 'head')
- grad_queries: bfloat16 [4096, 4096], P('seq', 'head')
- grad_keys: bfloat16 [4096, 4096], P('seq', 'head')
- grad_values: bfloat16 [4096, 4096], P('seq', 'head')
- grad_weight: float32 [4096, 4096], P('head', 'seq')
Inputs may be any that keep to these rules, and one draw needn't show every extreme that they name: `doc_block`: document numbers never fall along the blocks; each document covers 1 to 16 blocks, one exactly 16.
All inputs are finite; a program needn't handle non-finite values.
Results may differ from a plain program's by a relative error of at most 0.0061.
Values may be sent and summed in bfloat16 or wider, within the bound.
A program may use at most 192 MiB of HBM per device.

v0:
```python
import jax
import jax.numpy as jnp
from jax import lax
from jax.sharding import PartitionSpec as P

HD = 128
BLK = 128


def carried_in(value, axis, join, neutral, backward):
    count, mine = (lax.axis_size(axis), lax.axis_index(axis))
    pieces = jax.tree.map(lambda part: lax.all_gather(part, axis), value)
    if backward:
        pieces = jax.tree.map(lambda part: part[::-1], pieces)
        mine = count - 1 - mine
    so_far = jax.tree.map(
        lambda part, zero: jnp.full_like(part, 0) + jnp.asarray(zero, part.dtype), value, neutral
    )

    def lap(position, so_far):
        longer = join(so_far, jax.tree.map(lambda part: part[position], pieces))
        return jax.tree.map(lambda new, old: jnp.where(position < mine, new, old), longer, so_far)

    return lax.fori_loop(0, count - 1, lap, so_far)


def link_states(earlier, later):
    state_early, doc_early = earlier
    state_late, doc_late = later
    joined = state_late + jnp.where(doc_early == doc_late, state_early, jnp.zeros_like(state_early))
    return (
        jnp.where(doc_late < 0, state_early, joined),
        jnp.where(doc_late < 0, doc_early, doc_late),
    )


def body(queries, key_rows, value_rows, doc_block, out_weight, grad_output):
    hi = lax.Precision.HIGHEST
    factor = 1.0 / HD
    tokens_here = queries.shape[0]
    width_here = queries.shape[1]
    heads_here = width_here // HD
    block_count = tokens_here // BLK
    query_blocks = queries.reshape(block_count, BLK, heads_here, HD)
    key_blocks = key_rows.reshape(block_count, BLK, heads_here, HD)
    value_blocks = value_rows.reshape(block_count, BLK, heads_here, HD)
    causal = jnp.tril(jnp.ones((BLK, BLK), dtype=bool))
    scores = (
        jnp.einsum("nthd,nshd->nhts", query_blocks, key_blocks, preferred_element_type=jnp.float32)
        * factor
    )
    probs = jnp.where(causal, scores, 0.0).astype(jnp.bfloat16)
    block_states = jnp.einsum(
        "nshd,nshe->nhde", key_blocks, value_blocks, preferred_element_type=jnp.float32
    )
    grad_att = lax.dot_general(
        grad_output, out_weight, (((1,), (1,)), ((), ())), preferred_element_type=jnp.float32
    ).astype(jnp.bfloat16)
    grad_blocks = grad_att.reshape(block_count, BLK, heads_here, HD)
    grad_states = jnp.einsum(
        "nthd,nthe->nhde", query_blocks, grad_blocks, preferred_element_type=jnp.float32
    )
    positions = jnp.arange(block_count, dtype=jnp.int32)
    same_doc = doc_block[:, None] == doc_block[None, :]
    earlier = (same_doc & (positions[None, :] < positions[:, None])).astype(jnp.float32)
    later = (same_doc & (positions[None, :] > positions[:, None])).astype(jnp.float32)
    last_doc = doc_block[block_count - 1]
    first_doc = doc_block[0]
    own_state = jnp.einsum(
        "c,chde->hde", (doc_block == last_doc).astype(jnp.float32), block_states, precision=hi
    )
    own_grad = jnp.einsum(
        "c,chde->hde", (doc_block == first_doc).astype(jnp.float32), grad_states, precision=hi
    )
    blank = jnp.zeros_like(own_state)
    carry_state, carry_doc = carried_in(
        (own_state, last_doc), "seq", link_states, (blank, jnp.int32(-1)), False
    )
    carry_grad, grad_doc = carried_in(
        (own_grad, first_doc), "seq", link_states, (blank, jnp.int32(-1)), True
    )
    before = jnp.einsum("bc,chde->bhde", earlier, block_states, precision=hi)
    before = before + jnp.where(
        (doc_block == carry_doc)[:, None, None, None], carry_state[None], 0.0
    )
    after = jnp.einsum("bc,chde->bhde", later, grad_states, precision=hi)
    after = after + jnp.where((doc_block == grad_doc)[:, None, None, None], carry_grad[None], 0.0)
    query_wide = query_blocks.astype(jnp.float32)
    attended = jnp.einsum(
        "nhts,nshe->nthe", probs, value_blocks, preferred_element_type=jnp.float32
    )
    attended = attended + factor * jnp.einsum("nthd,nhde->nthe", query_wide, before, precision=hi)
    attended = attended.astype(jnp.bfloat16).reshape(tokens_here, width_here)
    partial_value = jnp.dot(attended, out_weight, preferred_element_type=jnp.float32)
    partial_value = lax.optimization_barrier(partial_value.astype(jnp.bfloat16))
    projected = lax.psum_scatter(
        partial_value.astype(jnp.float32).astype(jnp.bfloat16),
        "head",
        scatter_dimension=1,
        tiled=True,
    )
    weight_term = lax.dot_general(
        attended, grad_output, (((0,), (0,)), ((), ())), preferred_element_type=jnp.float32
    )
    grad_weight = lax.psum_scatter(weight_term, "seq", scatter_dimension=1, tiled=True)
    grad_scores = (
        jnp.einsum("nthe,nshe->nhts", grad_blocks, value_blocks, preferred_element_type=jnp.float32)
        * factor
    )
    grad_probs = jnp.where(causal, grad_scores, 0.0).astype(jnp.bfloat16)
    grad_queries = jnp.einsum(
        "nhts,nshd->nthd", grad_probs, key_blocks, preferred_element_type=jnp.float32
    )
    grad_queries = grad_queries + factor * jnp.einsum(
        "nthe,nhde->nthd", grad_blocks.astype(jnp.float32), before, precision=hi
    )
    grad_keys = jnp.einsum(
        "nhts,nthd->nshd", grad_probs, query_blocks, preferred_element_type=jnp.float32
    )
    grad_keys = grad_keys + factor * jnp.einsum(
        "nshe,nhde->nshd", value_blocks.astype(jnp.float32), after, precision=hi
    )
    grad_values = jnp.einsum(
        "nhts,nthe->nshe", probs, grad_blocks, preferred_element_type=jnp.float32
    )
    grad_values = grad_values + factor * jnp.einsum(
        "nshd,nhde->nshe", key_blocks.astype(jnp.float32), after, precision=hi
    )
    shape_out = (tokens_here, width_here)
    return (
        projected,
        grad_queries.astype(jnp.bfloat16).reshape(shape_out),
        grad_keys.astype(jnp.bfloat16).reshape(shape_out),
        grad_values.astype(jnp.bfloat16).reshape(shape_out),
        grad_weight,
    )


def solution(mesh):
    placed = (
        P("seq", "head"),
        P("seq", "head"),
        P("seq", "head"),
        P("seq"),
        P("head", None),
        P("seq", None),
    )
    return jax.shard_map(
        body,
        mesh=mesh,
        in_specs=placed,
        out_specs=(
            P("seq", "head"),
            P("seq", "head"),
            P("seq", "head"),
            P("seq", "head"),
            P("head", "seq"),
        ),
        check_vma=False,
    )
```

profile of v0, /device:TPU:0, one launch (start us, length us, event | category | flops | bytes accessed | tf_op | source)
XLA Modules:
  0.0 1211.4 jit_solution(17889509434576382787)
XLA Ops:
  13.8 8.2 fusion.7
  22.3 8.3 fusion.11
  38.5 4.1 copy.89
  42.6 7.2 fusion.50
  50.6 16.3 %all-reduce.2 = (s32[16]{0:T(128)S(1)}, s32[16]{0:T(128)S(1)}) all-reduce(s32[16]{0:T(128)S(1)} %get-tuple-element.300, s32[16]{0:T(128)S(1)} %slice_dynamic-update-slice_fusion), channel_id=1, replica_groups=mesh['seq'=16,'head'=2] {'seq'}, use_global_device_ids=true, to_apply=%add | all-reduce | flops 32 | bytes 256
  67.1 3.5 select_convert_fusion.1
  70.6 5.7 fusion.9
  76.3 140.2 %all-gather.5.cloned.1.call-done = f32[256,128,128]{2,1,0:T(8,128)} async-done(((f32[16,128,128]{2,1,0:T(8,128)}), f32[256,128,128]{2,1,0:T(8,128)}) %all-gather.5.cloned.1.call-update) | async-done | bytes 16777232 | tf_op jit(solution)/shard_map/all_gather | solution.py:12
  216.5 78.9 %while.32 = (s32[]{:T(128)}, f32[16,128,128]{2,1,0:T(8,128)}, s32[]{:T(128)}, s32[]{:T(128)}, s32[16]{0:T(128)S(1)}, /*index=5*/f32[16,16,128,128]{3,2,1,0:T(8,128)}, s32[]{:T(128)}, s32[]{:T(128)}) while((s32[]{:T(128)}, f32[16,128,128]{2,1,0:T(8,128)}, s32[]{:T(128)}, s32[]{:T(128)}, s32[16]{0:T(128)S(1)}, ...), condition=%wide.region_1.2_spmd.clone, body=%wide.region_0.1_spmd.clone.sunk | while | flops 1310728 | bytes 3145903 | solution.py:24
  223.3 2.7 select_select_fusion.4
  228.6 2.7 select_select_fusion.4
  233.9 2.7 select_select_fusion.4
  239.2 2.7 select_select_fusion.4
  244.5 2.7 select_select_fusion.4
  249.8 2.7 select_select_fusion.4
  255.0 2.7 select_select_fusion.4
  265.6 2.7 select_select_fusion.4
  276.2 2.7 select_select_fusion.4
  281.5 2.7 select_select_fusion.4
  292.0 2.8 select_select_fusion.4
  295.4 114.3 %all-gather.7.cloned.1.call-done = f32[256,128,128]{2,1,0:T(8,128)} async-done(((f32[16,128,128]{2,1,0:T(8,128)}), f32[256,128,128]{2,1,0:T(8,128)}) %all-gather.7.cloned.1.call-update) | async-done | bytes 16777232 | tf_op jit(solution)/shard_map/all_gather | solution.py:12
  409.7 11.6 rev.7
  421.3 64.8 %while.33 = (s32[]{:T(128)}, f32[16,128,128]{2,1,0:T(8,128)S(1)}, s32[]{:T(128)}, s32[]{:T(128)}, s32[16]{0:T(128)S(1)}, /*index=5*/f32[16,16,128,128]{3,2,1,0:T(8,128)}, s32[]{:T(128)}, s32[]{:T(128)}) while((s32[]{:T(128)}, f32[16,128,128]{2,1,0:T(8,128)S(1)}, s32[]{:T(128)}, s32[]{:T(128)}, s32[16]{0:T(128)S(1)}, ...), condition=%wide.region_4.5_spmd.clone, body=%wide.region_3.4_spmd.clone.sunk | while | flops 1310728 | bytes 3145903 | solution.py:24
  486.2 4.3 fusion.4
  495.0 11.9 convolution_convert_fusion
  507.3 14.7 %fusion.13 = f32[2048,4096]{1,0:T(8,128)} fusion(bf16[256,4096]{1,0:T(8,128)(2,1)S(1)} %copy-done, bf16[32,8,16,128]{3,2,1,0:T(8,128)(2,1)} %bitcast.130), kind=kOutput, calls=%fused_computation.31 | convolution fusion | flops 4294967296 | bytes 36700160 | tf_op jit(solution)/shard_map/dot_general | solution.py:102
  524.7 5.2 fusion.46
  538.4 3.4 fusion.5
  543.3 2.9 copy.96
  546.3 4.5 fusion.6
  553.1 3.4 copy_bitcast_fusion
  556.4 647.9 %reduce-scatter.5.cloned.1.call-done = f32[2048,256]{1,0:T(8,128)} async-done(((f32[2048,4096]{1,0:T(8,128)}), f32[2048,256]{1,0:T(8,128)}) %reduce-scatter.5.cloned.1.call-update) | async-done | bytes 2097168 | tf_op jit(solution)/shard_map/reduce_scatter | solution.py:105
  (129 shorter events, 89.7 us)
Async XLA Ops:
  7.2 15.1 %copy-start = (bf16[256,4096]{1,0:T(8,128)(2,1)S(1)}, bf16[256,4096]{1,0:T(8,128)(2,1)}, u32[]{:S(2)}) copy-start(bf16[256,4096]{1,0:T(8,128)(2,1)} %param.15) | copy-start | bytes 6291460
  7.2 1.7 copy-start.19
  7.2 209.3 %all-gather.5.cloned.1.call-start = ((), (), s32[]{:S(2)}) async-start(), calls=%async_computation.4 | async-start | bytes 17825792 | tf_op jit(solution)/shard_map/all_gather | solution.py:12
  8.9 1.0 copy-start.4
  9.1 1.0 copy-start.6
  10.2 1.9 copy-start.21
  10.2 2.5 copy-start.20
  22.0 387.7 %all-gather.7.cloned.1.call-start = ((), (), s32[]{:S(2)}) async-start(), calls=%async_computation.5 | async-start | bytes 17825792 | tf_op jit(solution)/shard_map/all_gather | solution.py:12
  33.7 4.7 copy-start.10
  35.6 1.1 copy-start.8
  49.9 506.6 %reduce-scatter.3.cloned.1.call-start = ((), (), s32[]{:S(2)}) async-start(), calls=%async_computation.2 | async-start | bytes 3145728 | tf_op jit(solution)/shard_map/reduce_scatter | solution.py:96
  67.1 3.5 copy-start.14
  486.2 4.3 copy-start.5
  486.2 4.3 copy-start.15
  507.0 697.4 %reduce-scatter.5.cloned.1.call-start = ((), (), s32[]{:S(2)}) async-start(), calls=%async_computation.3 | async-start | bytes 35651584 | tf_op jit(solution)/shard_map/reduce_scatter | solution.py:105
  522.0 2.6 copy-start.13
  524.6 6.6 copy-start.17
  524.6 5.2 copy-start.1
  524.6 5.2 copy-start.2
  524.6 5.2 copy-start.11
  529.9 1.4 copy-start.7
  535.8 2.6 copy-start.3
  538.4 3.4 copy-start.12
  538.4 3.4 copy-start.16
  546.2 4.5 copy-start.9
  546.3 4.5 copy-start.18
Sparse Core Ops, SparseCore 0:
  22.1 194.3 all-gather.4
  219.8 189.8 all-gather.6
  507.1 7.7 reduce-scatter.2
  522.1 682.1 reduce-scatter.4
where the time goes:
time: 1220 us; the launch traced here: 1210 us
  waiting for transfers between devices  903 us (74%)
  matrix products  90.3 us (7%)
  other arithmetic  66.8 us (5%)
  local copies, waits for them, and re-layouts  60.8 us (5%)
  loops' own time  59.4 us (5%)
  blocking collectives  16.3 us (1%)
  between operations  14.7 us (1%)
    reduce_scatter x1, waiting for transfers between devices, body(): lax.psum_scatter(weight_term, 'seq', scatter_dimension=1, tiled=True)  648 us
    all_gather x2, waiting for transfers between devices, carried_in(): pieces = jax.tree.map(lambda part: lax.all_gather(part, axis), value)  254 us
    select_n x30, other arithmetic, lap(): jnp.where(position < mine, new, old)  66.8 us
    another operation x2, loops' own time, carried_in(): return lax.fori_loop(0, count - 1, lap, so_far)  59.4 us
  transfers between devices with their start and end apart: 4, of which 3 were waited for; matrix products, arithmetic and copies ran while one was open for 11% of the time, Pallas kernels for 0%

commit v1 on v0

v1 whole, which is shorter than its diff:
```python
import jax
import jax.numpy as jnp
from jax import lax
from jax.sharding import PartitionSpec as P

HD = 128
BLK = 128


def row_groups(count):
    near = 1
    while near * near < count:
        near += 1
    while count % near:
        near += 1
    far = count // near
    rows = [[r * near + c for c in range(near)] for r in range(far)]
    columns = [[r * near + c for r in range(far)] for c in range(near)]
    return near, far, rows, columns


def over_blocks(mask, states):
    count = states.shape[0]
    picked = [
        sum(mask[b, c] * states[c] for c in range(count) if c != b) + jnp.zeros_like(states[0])
        for b in range(count)
    ]
    return jnp.stack(picked)


def carried(states, grads, first_doc, last_doc):
    count, mine = (lax.axis_size("seq"), lax.axis_index("seq"))
    ends = lax.all_gather(jnp.stack([first_doc, last_doc]), "seq")
    firsts, lasts = (ends[:, 0], ends[:, 1])
    heads = states.shape[0]
    rows = heads * HD // count
    both = jnp.stack([states, grads]).astype(jnp.bfloat16).reshape(2, count, rows, HD)
    both = jnp.moveaxis(both, 1, 0)
    got = lax.all_to_all(both, "seq", 0, 0).astype(jnp.float32)
    place = jnp.arange(count)
    ahead = ((lasts[None, :] == firsts[:, None]) & (place[None, :] < place[:, None])).astype(jnp.float32)
    behind = ((firsts[None, :] == lasts[:, None]) & (place[None, :] > place[:, None])).astype(jnp.float32)
    masks = jnp.stack([ahead, behind])
    summed = [jnp.sum(masks[:, j, :].T[:, :, None, None] * got, axis=0) for j in range(count)]
    summed = jnp.stack(summed).astype(jnp.bfloat16)
    back = lax.all_to_all(summed, "seq", 0, 0)
    back = jnp.moveaxis(back, 0, 1).reshape(2, heads, HD, HD).astype(jnp.float32)
    return back[0], back[1]


def body(queries, key_rows, value_rows, doc_block, out_weight, grad_output):
    factor = 1.0 / HD
    tokens_here = queries.shape[0]
    width_here = queries.shape[1]
    heads_here = width_here // HD
    block_count = tokens_here // BLK
    query_blocks = queries.reshape(block_count, BLK, heads_here, HD)
    key_blocks = key_rows.reshape(block_count, BLK, heads_here, HD)
    value_blocks = value_rows.reshape(block_count, BLK, heads_here, HD)
    near, far, rows, columns = row_groups(lax.axis_size("seq"))
    near_out = lax.all_to_all(
        grad_output.reshape(tokens_here, far, near, -1), "seq", 2, 0, axis_index_groups=rows
    ).reshape(near * tokens_here, -1)
    causal = jnp.tril(jnp.ones((BLK, BLK), dtype=bool))
    scores = (
        jnp.einsum("nthd,nshd->nhts", query_blocks, key_blocks, preferred_element_type=jnp.float32)
        * factor
    )
    probs = jnp.where(causal, scores, 0.0).astype(jnp.bfloat16)
    block_states = jnp.einsum(
        "nshd,nshe->nhde", key_blocks, value_blocks, preferred_element_type=jnp.float32
    )
    grad_att = lax.dot_general(
        grad_output, out_weight, (((1,), (1,)), ((), ())), preferred_element_type=jnp.float32
    ).astype(jnp.bfloat16)
    grad_blocks = grad_att.reshape(block_count, BLK, heads_here, HD)
    grad_states = jnp.einsum(
        "nthd,nthe->nhde", query_blocks, grad_blocks, preferred_element_type=jnp.float32
    )
    positions = jnp.arange(block_count, dtype=jnp.int32)
    same_doc = doc_block[:, None] == doc_block[None, :]
    earlier = (same_doc & (positions[None, :] < positions[:, None])).astype(jnp.float32)
    later = (same_doc & (positions[None, :] > positions[:, None])).astype(jnp.float32)
    last_doc = doc_block[block_count - 1]
    first_doc = doc_block[0]
    own_state = jnp.sum(
        jnp.where((doc_block == last_doc)[:, None, None, None], block_states, 0.0), axis=0
    )
    own_grad = jnp.sum(
        jnp.where((doc_block == first_doc)[:, None, None, None], grad_states, 0.0), axis=0
    )
    carry_state, carry_grad = carried(own_state, own_grad, first_doc, last_doc)
    before = over_blocks(earlier, block_states)
    before = before + jnp.where(
        (doc_block == first_doc)[:, None, None, None], carry_state[None], 0.0
    )
    after = over_blocks(later, grad_states)
    after = after + jnp.where((doc_block == last_doc)[:, None, None, None], carry_grad[None], 0.0)
    before = before.astype(jnp.bfloat16)
    after = after.astype(jnp.bfloat16)
    attended = jnp.einsum(
        "nhts,nshe->nthe", probs, value_blocks, preferred_element_type=jnp.float32
    )
    attended = attended + factor * jnp.einsum("nthd,nhde->nthe", query_blocks, before, preferred_element_type=jnp.float32)
    attended = attended.astype(jnp.bfloat16).reshape(tokens_here, width_here)
    partial_value = jnp.dot(attended, out_weight, preferred_element_type=jnp.float32)
    partial_value = lax.optimization_barrier(partial_value.astype(jnp.bfloat16))
    projected = lax.psum_scatter(
        partial_value.astype(jnp.float32).astype(jnp.bfloat16),
        "head",
        scatter_dimension=1,
        tiled=True,
    )
    near_att = lax.all_gather(attended, "seq", axis_index_groups=rows, tiled=True)
    weight_term = lax.dot_general(
        near_att, near_out, (((0,), (0,)), ((), ())), preferred_element_type=jnp.float32
    ).astype(jnp.bfloat16)
    weight_parts = lax.all_to_all(
        weight_term.reshape(width_here, far, -1),
        "seq",
        1,
        0,
        axis_index_groups=columns,
    )
    grad_weight = jnp.sum(weight_parts.astype(jnp.float32), axis=0)
    grad_scores = (
        jnp.einsum("nthe,nshe->nhts", grad_blocks, value_blocks, preferred_element_type=jnp.float32)
        * factor
    )
    grad_probs = jnp.where(causal, grad_scores, 0.0).astype(jnp.bfloat16)
    grad_queries = jnp.einsum(
        "nhts,nshd->nthd", grad_probs, key_blocks, preferred_element_type=jnp.float32
    )
    grad_queries = grad_queries + factor * jnp.einsum(
        "nthe,nhde->nthd", grad_blocks, before, preferred_element_type=jnp.float32
    )
    grad_keys = jnp.einsum(
        "nhts,nthd->nshd", grad_probs, query_blocks, preferred_element_type=jnp.float32
    )
    grad_keys = grad_keys + factor * jnp.einsum(
        "nshe,nhde->nshd", value_blocks, after, preferred_element_type=jnp.float32
    )
    grad_values = jnp.einsum(
        "nhts,nthe->nshe", probs, grad_blocks, preferred_element_type=jnp.float32
    )
    grad_values = grad_values + factor * jnp.einsum(
        "nshd,nhde->nshe", key_blocks, after, preferred_element_type=jnp.float32
    )
    shape_out = (tokens_here, width_here)
    return (
        projected,
        grad_queries.astype(jnp.bfloat16).reshape(shape_out),
        grad_keys.astype(jnp.bfloat16).reshape(shape_out),
        grad_values.astype(jnp.bfloat16).reshape(shape_out),
        grad_weight,
    )


def solution(mesh):
    placed = (
        P("seq", "head"),
        P("seq", "head"),
        P("seq", "head"),
        P("seq"),
        P("head", None),
        P("seq", None),
    )
    return jax.shard_map(
        body,
        mesh=mesh,
        in_specs=placed,
        out_specs=(
            P("seq", "head"),
            P("seq", "head"),
            P("seq", "head"),
            P("seq", "head"),
            P("head", "seq"),
        ),
        check_vma=False,
    )
```

time: 1220 us -> 322 us (0.26)
  waiting for transfers between devices: 903 us -> 96 us
  loops' own time: 59.4 us -> 0 us
  blocking collectives: 16.3 us -> 61 us
  other arithmetic: 66.8 us -> 23.5 us
  matrix products: 90.3 us -> 52.2 us
  starting transfers between devices: 0.59 us -> 18.3 us
    reduce_scatter x1 -> x0, waiting for transfers between devices: 648 us -> none  [body(): lax.psum_scatter(weight_term, 'seq', scatter_dimension=1, tiled=True)]
    all_gather x2 -> x1, waiting for transfers between devices: 254 us -> 26.4 us  [body(): lax.all_gather(attended, 'seq', axis_index_groups=rows, tiled=True)]
    all_to_all x0 -> x3, waiting for transfers between devices: none -> 69.5 us  [the longest x1 54.9 us: body(): lax.all_to_all(weight_term.reshape(width_here, far, -1), 'seq', 1, 0, axi...]
    select_n x30 -> x0, other arithmetic: 66.8 us -> none  [lap(): jnp.where(position < mine, new, old)]
    another operation x2 -> x0, loops' own time: 59.4 us -> none  [carried_in(): return lax.fori_loop(0, count - 1, lap, so_far)]
    dot_general x9 -> x5, matrix products: 54.6 us -> 15.7 us  [the longest x1 9.35 us: body(): lax.dot_general(near_att, near_out, (((0,), (0,)), ((), ())), preferred_e...]
    all_to_all x0 -> x1, blocking collectives: none -> 36.7 us  [body(): lax.all_to_all(grad_output.reshape(tokens_here, far, near, -1), 'seq', 2,...]
    unnamed x53 -> x65, local copies, waits for them, and re-layouts: 11 us -> 33.7 us
  transfers between devices with their start and end apart: 4 -> 5, of which waited for: 3 -> 3; matrix products, arithmetic and copies ran while one was open for 11% -> 19% of each run, Pallas kernels for 0% -> 0%
where the time goes in v1:
time: 322 us; the launch traced here: 320 us
  waiting for transfers between devices  96 us (30%)
  blocking collectives  61 us (19%)
  local copies, waits for them, and re-layouts  52.8 us (16%)
  matrix products  52.2 us (16%)
  other arithmetic  23.5 us (7%)
  starting transfers between devices  18.3 us (6%)
  between operations  16.5 us (5%)
    all_to_all x1, waiting for transfers between devices, body(): lax.all_to_all(weight_term.reshape(width_here, far, -1), 'seq', 1, 0, axi...  54.9 us
    all_to_all x1, blocking collectives, body(): lax.all_to_all(grad_output.reshape(tokens_here, far, near, -1), 'seq', 2,...  36.7 us
    unnamed x65, local copies, waits for them, and re-layouts  33.7 us
    all_gather x1, waiting for transfers between devices, body(): lax.all_gather(attended, 'seq', axis_index_groups=rows, tiled=True)  26.4 us
    unnamed x1, blocking collectives  24.3 us
    all_to_all x1, waiting for transfers between devices, carried(): back = lax.all_to_all(summed, 'seq', 0, 0)  14.6 us
    dot_general x1, matrix products, body(): lax.dot_general(grad_output, out_weight, (((1,), (1,)), ((), ())), prefer...  11.9 us
    dot_general x1, matrix products, body(): jnp.dot(attended, out_weight, preferred_element_type=jnp.float32)  11.9 us
  transfers between devices with their start and end apart: 5, of which 3 were waited for; matrix products, arithmetic and copies ran while one was open for 19% of the time, Pallas kernels for 0%

profile of v1, /device:TPU:0, one launch (start us, length us, event | category | flops | bytes accessed | tf_op | source)
XLA Modules:
  0.0 320.4 jit_solution(1472348763524654234)
XLA Ops:
  10.9 11.9 %fusion.21 = bf16[32,8,16,128]{3,1,2,0:T(8,128)(2,1)} fusion(bf16[256,4096]{1,0:T(8,128)(2,1)} %param.11, bf16[2048,4096]{1,0:T(8,128)(2,1)} %param.10), kind=kOutput, calls=%fused_computation.53 | convolution fusion | flops 4295491584 | bytes 19922944 | tf_op jit(solution)/shard_map/dot_general | solution.py:73
  22.8 2.4 copy.246
  25.3 2.6 copy.195
  29.2 2.0 select_reduce_fusion.1
  31.2 2.3 select_reduce_fusion
  34.6 8.4 %all-to-all-start = ((bf16[16,2,128,128]{3,2,1,0:T(8,128)(2,1)}), bf16[16,2,128,128]{3,2,1,0:T(8,128)(2,1)}, u32[]{:S(2)}, u32[]{:S(2)}) async-start(bf16[16,2,128,128]{3,2,1,0:T(8,128)(2,1)} %maximum_bitcast_fusion), calls=%async_computation | async-start | bytes 2097152 | tf_op jit(solution)/shard_map/all_to_all | solution.py:39
  44.5 24.3 %all-reduce = s32[32]{0:T(128)S(1)} all-reduce(s32[32]{0:T(128)S(1)} %dynamic-update-slice), channel_id=2, replica_groups=mesh['seq'=16,'head'=2] {'seq'}, use_global_device_ids=true, to_apply=%add | all-reduce | flops 32 | bytes 256
  70.5 5.4 %fusion.15 = (bf16[2,128,128]{2,1,0:T(8,128)(2,1)S(1)}, bf16[2,128,128]{2,1,0:T(8,128)(2,1)S(1)}, bf16[2,128,128]{2,1,0:T(8,128)(2,1)S(1)}, bf16[2,128,128]{2,1,...) fusion(bf16[16,2,128,128]{3,2,1,0:T(8,128)(2,1)} %all-to-all-do, ...), kind=kLoop, calls=%fused_computation.35 | loop fusion | flops 16777216 | bytes 2099200 | tf_op jit(solution)/shard_map/reduce_sum | solution.py:44
  85.9 4.6 %all-to-all-start.1 = ((bf16[16,2,128,128]{3,2,1,0:T(8,128)(2,1)}), bf16[16,2,128,128]{3,2,1,0:T(8,128)(2,1)}, u32[]{:S(2)}, u32[]{:S(2)}) async-start(bf16[16,2,128,128]{3,2,1,0:T(8,128)(2,1)} %bitcast_dynamic-update-slice_fusion), calls=%async_computation.1 | async-start | bytes 2097152 | tf_op jit(solution)/shard_map/all_to_all | solution.py:46
  91.6 4.4 %slice_multiply_fusion.3 = (f32[1,16,128,128]{3,2,1,0:T(8,128)}, f32[1,16,128,128]{3,2,1,0:T(8,128)}) fusion(f32[2,16,128,128]{3,2,1,0:T(8,128)} %get-tuple-element.75, f32[]{:T(128)} %bitcast.1, f32[]{:T(128)} %bitcast.2), kind=kLoop, calls=%fused_computation.64 | loop fusion | flops 524288 | bytes 4194312 | tf_op jit(solution)/shard_map/mul | solution.py:25
  97.8 2.2 fusion.29
  100.0 14.6 %all-to-all-done.1 = bf16[16,2,128,128]{3,2,1,0:T(8,128)(2,1)} async-done(((bf16[16,2,128,128]{3,2,1,0:T(8,128)(2,1)}), bf16[16,2,128,128]{3,2,1,0:T(8,128)(2,1)}, u32[]{:S(2)}, u32[]{:S(2)}) %all-to-all-start.1) | async-done | bytes 1048608 | tf_op jit(solution)/shard_map/all_to_all | solution.py:46
  119.9 1.9 fusion.20
  121.8 2.6 copy.215
  124.4 2.5 copy.294
  126.9 4.1 %copy.231 = bf16[256,4096]{0,1:T(8,128)(2,1)} copy(bf16[256,4096]{1,0:T(8,128)(2,1)} %param.11) | data formatting | bytes 4194304 | tf_op args[5]
  131.0 4.3 %copy.232 = bf16[1,256,4,4,256]{4,2,1,0,3:T(4,128)(2,1)} copy(bf16[1,256,4,4,256]{1,4,3,2,0:T(8,128)(2,1)} %bitcast.218) | data formatting | bytes 4194304 | tf_op jit(solution)/shard_map/broadcast_in_dim;reshape | solution.py:61
  135.3 36.7 %all_to_all.34 = bf16[1,256,4,4,256]{4,2,1,0,3:T(4,128)(2,1)S(1)} all-to-all(bf16[1,256,4,4,256]{4,2,1,0,3:T(4,128)(2,1)} %copy.232), channel_id=1, replica_groups={{0,2,4,6},{8,10,12,14},{16,18,20,22},{24,26,28,30},{1,3,5,7},{9,11,13,1..., dimensions={3} | all-to-all | bytes 4194304 | tf_op jit(solution)/shard_map/all_to_all | solution.py:61
  172.1 1.8 copy.251
  173.9 26.4 %all-gather.3.cloned.1.call-done = bf16[1024,2048]{1,0:T(8,128)(2,1)} async-done(((bf16[256,2048]{1,0:T(8,128)(2,1)}), bf16[1024,2048]{1,0:T(8,128)(2,1)}) %all-gather.3.cloned.1.call-update) | async-done | bytes 4194320 | tf_op jit(solution)/shard_map/all_gather | solution.py:114
  200.3 9.3 %convolution_convert_fusion.1 = bf16[2048,1024]{0,1:T(8,128)(2,1)} fusion(bf16[1024,2048]{1,0:T(8,128)(2,1)} %all-gather.3.cloned.1.call-done, bf16[1024,1024]{1,0:T(8,128)(2,1)} %bitcast.226), kind=kOutput, calls=%fused_computation.18 | convolution fusion | flops 4297064448 | bytes 10485760 | tf_op jit(solution)/shard_map/dot_general | solution.py:115
  209.6 4.8 %all-to-all-start.3 = ((bf16[1,2048,4,256]{1,3,0,2:T(8,128)(2,1)}), bf16[1,2048,4,256]{1,3,0,2:T(8,128)(2,1)}, u32[]{:S(2)}, u32[]{:S(2)}) async-start(bf16[1,2048,4,256]{1,3,0,2:T(8,128)(2,1)} %bitcast.219), calls=%async_computation.4 | async-start | bytes 8388608 | tf_op jit(solution)/shard_map/all_to_all | solution.py:118
  214.8 11.9 %convolution_convert_fusion = bf16[256,4096]{1,0:T(8,128)(2,1)} fusion(bf16[2048,4096]{1,0:T(8,128)(2,1)} %param.10, bf16[32,8,16,128]{3,2,1,0:T(8,128)(2,1)} %bitcast.221), kind=kOutput, calls=%fused_computation.17 | convolution fusion | flops 4296015872 | bytes 19922944 | tf_op jit(solution)/shard_map/dot_general | solution.py:106
  226.7 4.4 %slice_multiply_fusion.1 = (f32[1,16,128,128]{3,2,1,0:T(8,128)}, f32[1,16,128,128]{3,2,1,0:T(8,128)}) fusion(f32[2,16,128,128]{3,2,1,0:T(8,128)} %get-tuple-element.73, f32[]{:T(128)} %bitcast.64, f32[]{:T(128)} %bitcast.65), kind=kLoop, calls=%fused_computation.61 | loop fusion | flops 524288 | bytes 4194312 | tf_op jit(solution)/shard_map/mul | solution.py:25
  232.9 1.8 fusion.36
  234.9 1.8 fusion.46
  238.5 1.9 copy.221
  244.2 1.8 fusion.18
  246.1 1.9 copy.226
  253.1 54.9 %all-to-all-done.3 = bf16[1,2048,4,256]{1,3,0,2:T(8,128)(2,1)} async-done(((bf16[1,2048,4,256]{1,3,0,2:T(8,128)(2,1)}), bf16[1,2048,4,256]{1,3,0,2:T(8,128)(2,1)}, u32[]{:S(2)}, u32[]{:S(2)}) %all-to-all-start.3) | async-done | bytes 4194336 | tf_op jit(solution)/shard_map/all_to_all | solution.py:118
  308.0 3.2 convert_reduce_fusion
  311.1 1.8 copy.235
  (104 shorter events, 38.7 us)
Async XLA Ops:
  8.0 1.6 copy-start.14
  8.0 1.9 copy-start.15
  9.6 0.7 copy-start.16
  29.2 2.0 copy-start.3
  33.5 9.5 %copy-start.17 = (u32[32]{0:T(128)S(1)}, u32[32]{0:T(128)}, u32[]{:S(2)}) copy-start(u32[32]{0:T(128)} %constant.11) | copy-start | bytes 388
  34.6 35.9 %all-to-all-start = ((bf16[16,2,128,128]{3,2,1,0:T(8,128)(2,1)}), bf16[16,2,128,128]{3,2,1,0:T(8,128)(2,1)}, u32[]{:S(2)}, u32[]{:S(2)}) async-start(bf16[16,2,128,128]{3,2,1,0:T(8,128)(2,1)} %maximum_bitcast_fusion), calls=%async_computation | async-start | bytes 2097152 | tf_op jit(solution)/shard_map/all_to_all | solution.py:39
  85.9 28.7 %all-to-all-start.1 = ((bf16[16,2,128,128]{3,2,1,0:T(8,128)(2,1)}), bf16[16,2,128,128]{3,2,1,0:T(8,128)(2,1)}, u32[]{:S(2)}, u32[]{:S(2)}) async-start(bf16[16,2,128,128]{3,2,1,0:T(8,128)(2,1)} %bitcast_dynamic-update-slice_fusion), calls=%async_computation.1 | async-start | bytes 2097152 | tf_op jit(solution)/shard_map/all_to_all | solution.py:46
  90.6 109.7 %all-gather.3.cloned.1.call-start = ((), (), s32[]{:S(2)}) async-start(), calls=%async_computation.6 | async-start | bytes 5242880 | tf_op jit(solution)/shard_map/all_gather | solution.py:114
  96.8 1.0 copy-start.12
  116.0 1.5 copy-start.10
  116.1 1.9 copy-start.11
  118.0 2.0 copy-start.7
  118.3 1.0 copy-start
  209.6 98.3 %all-to-all-start.3 = ((bf16[1,2048,4,256]{1,3,0,2:T(8,128)(2,1)}), bf16[1,2048,4,256]{1,3,0,2:T(8,128)(2,1)}, u32[]{:S(2)}, u32[]{:S(2)}) async-start(bf16[1,2048,4,256]{1,3,0,2:T(8,128)(2,1)} %bitcast.219), calls=%async_computation.4 | async-start | bytes 8388608 | tf_op jit(solution)/shard_map/all_to_all | solution.py:118
  214.5 98.5 %reduce-scatter.2.cloned.1.call-start = ((), (), s32[]{:S(2)}) async-start(), calls=%async_computation.5 | async-start | bytes 3145728 | tf_op jit(solution)/shard_map/reduce_scatter | solution.py:108
  226.7 4.4 %copy-start.2 = (bf16[32,8,16,128]{3,2,1,0:T(8,128)(2,1)S(1)}, bf16[32,8,16,128]{3,2,1,0:T(8,128)(2,1)}, u32[]{:S(2)}) copy-start(bf16[32,8,16,128]{3,2,1,0:T(8,128)(2,1)} %copy.246) | copy-start | bytes 3145732
  232.9 1.9 copy-start.4
  232.9 2.0 copy-start.13
  234.8 1.8 copy-start.1
  240.4 1.3 copy-start.8
  240.4 1.9 copy-start.9
  242.3 1.9 copy-start.6
  248.0 2.0 copy-start.5
Sparse Core Ops, SparseCore 0:
  127.0 73.1 all-gather.2
Sparse Core Ops, SparseCore 1:
  226.8 9.7 reduce-scatter.1

commit v2 on v1

--- a/solution.py
+++ b/solution.py
@@ -14,9 +14,37 @@
     while count % near:
         near += 1
     far = count // near
-    rows = [[r * near + c for c in range(near)] for r in range(far)]
-    columns = [[r * near + c for r in range(far)] for c in range(near)]
-    return near, far, rows, columns
+    return near, far
+
+
+def swapped(near, far, step):
+    return [(r * near + c, r * near + (c ^ step)) for r in range(far) for c in range(near)]
+
+
+def column_sum(term, near, far):
+    row = lax.axis_index("seq") // near
+    wide = term.shape[1] // far
+
+    def block(place):
+        start = jnp.clip(place, 0, far - 1) * wide
+        return lax.dynamic_slice_in_dim(term, start, wide, 1)
+
+    up, down = (None, None)
+    for step in range(1, far):
+        climb = block(row + far - step)
+        sink = block(row - far + step)
+        if step > 1:
+            climb = climb + up.astype(jnp.float32)
+            sink = sink + down.astype(jnp.float32)
+        rising = [(r * near + c, (r + 1) * near + c) for r in range(step) for c in range(near)]
+        falling = [
+            ((far - 1 - r) * near + c, (far - 2 - r) * near + c)
+            for r in range(step)
+            for c in range(near)
+        ]
+        up = lax.ppermute(climb.astype(jnp.bfloat16), "seq", rising)
+        down = lax.ppermute(sink.astype(jnp.bfloat16), "seq", falling)
+    return block(row) + up.astype(jnp.float32) + down.astype(jnp.float32)
 
 
 def over_blocks(mask, states):
@@ -30,7 +58,9 @@
 
 def carried(states, grads, first_doc, last_doc):
     count, mine = (lax.axis_size("seq"), lax.axis_index("seq"))
-    ends = lax.all_gather(jnp.stack([first_doc, last_doc]), "seq")
+    ends = lax.all_to_all(
+        jnp.broadcast_to(jnp.stack([first_doc, last_doc]), (count, 2)), "seq", 0, 0
+    )
     firsts, lasts = (ends[:, 0], ends[:, 1])
     heads = states.shape[0]
     rows = heads * HD // count
@@ -57,10 +87,17 @@
     query_blocks = queries.reshape(block_count, BLK, heads_here, HD)
     key_blocks = key_rows.reshape(block_count, BLK, heads_here, HD)
     value_blocks = value_rows.reshape(block_count, BLK, heads_here, HD)
-    near, far, rows, columns = row_groups(lax.axis_size("seq"))
-    near_out = lax.all_to_all(
-        grad_output.reshape(tokens_here, far, near, -1), "seq", 2, 0, axis_index_groups=rows
-    ).reshape(near * tokens_here, -1)
+    near, far = row_groups(lax.axis_size("seq"))
+    seat = lax.axis_index("seq") % near
+    out_parts = grad_output.reshape(tokens_here, far, near, -1)
+
+    def out_part(place):
+        part = lax.dynamic_index_in_dim(out_parts, place, 2, keepdims=False)
+        return part.reshape(tokens_here, -1)
+
+    near_out = [out_part(seat)]
+    for step in range(1, near):
+        near_out.append(lax.ppermute(out_part(seat ^ step), "seq", swapped(near, far, step)))
     causal = jnp.tril(jnp.ones((BLK, BLK), dtype=bool))
     scores = (
         jnp.einsum("nthd,nshd->nhts", query_blocks, key_blocks, preferred_element_type=jnp.float32)
@@ -111,18 +148,20 @@
         scatter_dimension=1,
         tiled=True,
     )
-    near_att = lax.all_gather(attended, "seq", axis_index_groups=rows, tiled=True)
-    weight_term = lax.dot_general(
-        near_att, near_out, (((0,), (0,)), ((), ())), preferred_element_type=jnp.float32
-    ).astype(jnp.bfloat16)
-    weight_parts = lax.all_to_all(
-        weight_term.reshape(width_here, far, -1),
-        "seq",
-        1,
-        0,
-        axis_index_groups=columns,
-    )
-    grad_weight = jnp.sum(weight_parts.astype(jnp.float32), axis=0)
+    near_att = [attended]
+    for step in range(1, near):
+        near_att.append(lax.ppermute(attended, "seq", swapped(near, far, step)))
+    half = near // 2
+    weight_term = sum(
+        lax.dot_general(
+            jnp.concatenate(near_att[at : at + half]),
+            jnp.concatenate(near_out[at : at + half]),
+            (((0,), (0,)), ((), ())),
+            preferred_element_type=jnp.float32,
+        )
+        for at in range(0, near, half)
+    )
+    grad_weight = column_sum(weight_term, near, far)
     grad_scores = (
         jnp.einsum("nthe,nshe->nhts", grad_blocks, value_blocks, preferred_element_type=jnp.float32)
         * factor

time: 322 us -> 343 us (1.065)
  blocking collectives: 61 us -> 0 us
  waiting for transfers between devices: 96 us -> 136 us
  starting transfers between devices: 18.3 us -> 49.6 us
  other arithmetic: 23.5 us -> 33.1 us
    ppermute x0 -> x12, waiting for transfers between devices: none -> 103 us  [the longest x3 54.7 us: body(): lax.ppermute(out_part(seat ^ step), 'seq', swapped(near, far, step))]
    all_to_all x1, waiting for transfers between devices: 54.9 us -> 0.01 us  [carried(): lax.all_to_all(jnp.broadcast_to(jnp.stack([first_doc, last_doc]), (count,...]
    all_to_all x1 -> x0, blocking collectives: 36.7 us -> none  [body(): lax.all_to_all(grad_output.reshape(tokens_here, far, near, -1), 'seq', 2,...]
    ppermute x0 -> x12, starting transfers between devices: none -> 28.2 us  [the longest x3 17.2 us: column_sum(): up = lax.ppermute(climb.astype(jnp.bfloat16), 'seq', rising)]
    all_gather x1 -> x0, waiting for transfers between devices: 26.4 us -> none  [body(): lax.all_gather(attended, 'seq', axis_index_groups=rows, tiled=True)]
    unnamed x1 -> x0, blocking collectives: 24.3 us -> none
    all_to_all x1, waiting for transfers between devices: 0.01 us -> 22.3 us  [carried(): got = lax.all_to_all(both, 'seq', 0, 0).astype(jnp.float32)]
    convert_element_type x1 -> x3, other arithmetic: 1.72 us -> 10.9 us  [the longest x2 7.81 us: column_sum(): up = lax.ppermute(climb.astype(jnp.bfloat16), 'seq', rising)]
  transfers between devices with their start and end apart: 5 -> 16, of which waited for: 3 -> 7; matrix products, arithmetic and copies ran while one was open for 19% -> 29% of each run, Pallas kernels for 0% -> 0%
where the time goes in v2:
time: 343 us; the launch traced here: 342 us
  waiting for transfers between devices  136 us (40%)
  local copies, waits for them, and re-layouts  55.5 us (16%)
  matrix products  53 us (15%)
  starting transfers between devices  49.6 us (14%)
  other arithmetic  33.1 us (10%)
  between operations  14.4 us (4%)
    ppermute x3, waiting for transfers between devices, body(): lax.ppermute(out_part(seat ^ step), 'seq', swapped(near, far, step))  54.7 us
    unnamed x74, local copies, waits for them, and re-layouts  34.2 us
    ppermute x3, waiting for transfers between devices, column_sum(): up = lax.ppermute(climb.astype(jnp.bfloat16), 'seq', rising)  29.6 us
    all_to_all x1, waiting for transfers between devices, carried(): got = lax.all_to_all(both, 'seq', 0, 0).astype(jnp.float32)  22.3 us
    ppermute x3, waiting for transfers between devices, column_sum(): down = lax.ppermute(sink.astype(jnp.bfloat16), 'seq', falling)  19.1 us
    ppermute x3, starting transfers between devices, column_sum(): up = lax.ppermute(climb.astype(jnp.bfloat16), 'seq', rising)  17.2 us
    dot_general x1, matrix products, body(): lax.dot_general(grad_output, out_weight, (((1,), (1,)), ((), ())), prefer...  11.9 us
    dot_general x1, matrix products, body(): jnp.dot(attended, out_weight, preferred_element_type=jnp.float32)  11.4 us
  transfers between devices with their start and end apart: 16, of which 7 were waited for; matrix products, arithmetic and copies ran while one was open for 29% of the time, Pallas kernels for 0%

profile of v2, /device:TPU:0, one launch (start us, length us, event | category | flops | bytes accessed | tf_op | source)
XLA Modules:
  0.0 341.6 jit_solution(11692752576528081353)
XLA Ops:
  8.5 8.3 %all-to-all-start = ((s32[16,1,2]{2,1,0:T(1,128)}), s32[16,1,2]{2,1,0:T(1,128)S(1)}, u32[]{:S(2)}, u32[]{:S(2)}) async-start(s32[16,1,2]{2,1,0:T(1,128)} %broadcast_in_dim.96), calls=%async_computation | async-start | bytes 16384 | tf_op jit(solution)/shard_map/all_to_all | solution.py:61
  20.2 11.9 %fusion.28 = bf16[32,8,16,128]{3,1,2,0:T(8,128)(2,1)} fusion(bf16[256,4096]{1,0:T(8,128)(2,1)} %param.11, bf16[2048,4096]{1,0:T(8,128)(2,1)} %param.10), kind=kOutput, calls=%fused_computation.66 | convolution fusion | flops 4295491584 | bytes 19922944 | tf_op jit(solution)/shard_map/dot_general | solution.py:110
  34.5 2.6 copy.190
  43.7 7.0 %all-to-all-start.1 = ((bf16[16,2,128,128]{3,2,1,0:T(8,128)(2,1)}), bf16[16,2,128,128]{3,2,1,0:T(8,128)(2,1)}, u32[]{:S(2)}, u32[]{:S(2)}) async-start(bf16[16,2,128,128]{3,2,1,0:T(8,128)(2,1)} %maximum_bitcast_fusion), calls=%async_computation.1 | async-start | bytes 2097152 | tf_op jit(solution)/shard_map/all_to_all | solution.py:69
  52.3 22.3 %all-to-all-done.1 = bf16[16,2,128,128]{3,2,1,0:T(8,128)(2,1)} async-done(((bf16[16,2,128,128]{3,2,1,0:T(8,128)(2,1)}), bf16[16,2,128,128]{3,2,1,0:T(8,128)(2,1)}, u32[]{:S(2)}, u32[]{:S(2)}) %all-to-all-start.1) | async-done | bytes 1048608 | tf_op jit(solution)/shard_map/all_to_all | solution.py:69
  74.6 5.4 %fusion.15 = (bf16[2,128,128]{2,1,0:T(8,128)(2,1)S(1)}, bf16[2,128,128]{2,1,0:T(8,128)(2,1)S(1)}, bf16[2,128,128]{2,1,0:T(8,128)(2,1)S(1)}, bf16[2,128,128]{2,1,...) fusion(bf16[16,2,128,128]{3,2,1,0:T(8,128)(2,1)} %all-to-all-do, ...), kind=kLoop, calls=%fused_computation.34 | loop fusion | flops 16777216 | bytes 2099200 | tf_op jit(solution)/shard_map/reduce_sum | solution.py:74
  90.0 5.9 %all-to-all-start.2 = ((bf16[16,2,128,128]{3,2,1,0:T(8,128)(2,1)}), bf16[16,2,128,128]{3,2,1,0:T(8,128)(2,1)}, u32[]{:S(2)}, u32[]{:S(2)}) async-start(bf16[16,2,128,128]{3,2,1,0:T(8,128)(2,1)} %bitcast_dynamic-update-slice_fusion), calls=%async_computation.2 | async-start | bytes 2097152 | tf_op jit(solution)/shard_map/all_to_all | solution.py:76
  97.4 4.5 %slice_multiply_fusion.3 = (f32[1,16,128,128]{3,2,1,0:T(8,128)}, f32[1,16,128,128]{3,2,1,0:T(8,128)}) fusion(f32[2,16,128,128]{3,2,1,0:T(8,128)} %get-tuple-element.68, f32[]{:T(128)} %bitcast.1, f32[]{:T(128)} %bitcast.2), kind=kLoop, calls=%fused_computation.77 | loop fusion | flops 524288 | bytes 4194312 | tf_op jit(solution)/shard_map/mul | solution.py:53
  101.9 2.7 slice_multiply_fusion.1
  108.7 10.3 %all-to-all-done.2 = bf16[16,2,128,128]{3,2,1,0:T(8,128)(2,1)} async-done(((bf16[16,2,128,128]{3,2,1,0:T(8,128)(2,1)}), bf16[16,2,128,128]{3,2,1,0:T(8,128)(2,1)}, u32[]{:S(2)}, u32[]{:S(2)}) %all-to-all-start.2) | async-done | bytes 1048608 | tf_op jit(solution)/shard_map/all_to_all | solution.py:76
  127.2 2.6 copy.210
  134.4 4.1 %copy.226 = bf16[256,4096]{0,1:T(8,128)(2,1)} copy(bf16[256,4096]{1,0:T(8,128)(2,1)} %param.11) | data formatting | bytes 4194304 | tf_op args[5]
  138.5 2.7 constant_dynamic-slice_fusion.3
  141.2 2.8 collective-permute-start.5
  144.7 26.1 %collective-permute-done.5 = bf16[256,1024]{0,1:T(8,128)(2,1)S(1)} collective-permute-done((bf16[256,1024]{0,1:T(8,128)(2,1)S(1)}, bf16[256,1024]{0,1:T(8,128)(2,1)S(1)}, u32[]{:S(2)}, u32[]{:S(2)}) %collective-permute-start.5) | collective-permute-done | bytes 524320 | tf_op jit(solution)/shard_map/ppermute | solution.py:100
  172.2 28.6 %collective-permute-done.4 = bf16[256,1024]{0,1:T(8,128)(2,1)} collective-permute-done((bf16[256,1024]{0,1:T(8,128)(2,1)}, bf16[256,1024]{0,1:T(8,128)(2,1)}, u32[]{:S(2)}, u32[]{:S(2)}) %collective-permute-start.4) | collective-permute-done | bytes 524320 | tf_op jit(solution)/shard_map/ppermute | solution.py:100
  200.8 4.3 %fusion.21 = f32[2048,1024]{1,0:T(8,128)S(1)} fusion(bf16[256,2048]{1,0:T(8,128)(2,1)} %collective-permute-done.3, bf16[256,2048]{1,0:T(8,128)(2,1)} %collective-permute-done.2, bf16[256,1024]{0,1:T(8,128)(2,1)} %copy-done.24, bf16[256,1024]{0,1:T(8,128)(2,1)} %collective-permute-done.4), kind=kOutput, calls=%fused_computation.42 | convolution fusion | flops 2153775104 | bytes 11534336 | tf_op jit(solution)/shard_map/dot_general | solution.py:156
  205.1 4.2 %convolution_add_fusion = f32[2048,1024]{1,0:T(8,128)S(1)} fusion(f32[2048,1024]{1,0:T(8,128)S(1)} %fusion.21, bf16[256,2048]{1,0:T(8,128)(2,1)} %collective-permute-done, bf16[256,2048]{1,0:T(8,128)(2,1)} %bitcast.194, bf16[256,1024]{0,1:T(8,128)(2,1)} %collective-permute-done.1, bf16[256,1024]{0,1:T(8,128)(2,1)S(1)} %bitcast.218), kind=kOutput, calls=%fused_computation.17 | convolution fusion | flops 2155872256 | bytes 19922944 | tf_op jit(solution)/shard_map/dot_general | solution.py:156
  209.3 3.2 copy-done
  214.1 6.7 %collective-permute-start.6 = (bf16[2048,256]{1,0:T(8,128)(2,1)}, bf16[2048,256]{1,0:T(8,128)(2,1)}, u32[]{:S(2)}, u32[]{:S(2)}) collective-permute-start(bf16[2048,256]{1,0:T(8,128)(2,1)} %get-tuple-element.23), channel_id=1, source_target_pairs={{0,8},{2,10},{4,12},{6,14},{1,9},{3,11},{5,13},{7,15}} | collective-permute-start | bytes 3145736 | tf_op jit(solution)/shard_map/ppermute | solution.py:45
  222.7 20.1 %collective-permute-done.6 = bf16[2048,256]{1,0:T(8,128)(2,1)} collective-permute-done((bf16[2048,256]{1,0:T(8,128)(2,1)}, bf16[2048,256]{1,0:T(8,128)(2,1)}, u32[]{:S(2)}, u32[]{:S(2)}) %collective-permute-start.6) | collective-permute-done | bytes 1048608 | tf_op jit(solution)/shard_map/ppermute | solution.py:45
  242.7 3.1 add_convert_fusion.3
  245.9 5.4 %collective-permute-start.7 = (bf16[2048,256]{1,0:T(8,128)(2,1)}, bf16[2048,256]{1,0:T(8,128)(2,1)}, u32[]{:S(2)}, u32[]{:S(2)}) collective-permute-start(bf16[2048,256]{1,0:T(8,128)(2,1)} %add_convert_fusion.3), channel_id=1, source_target_pairs={{0,8},{2,10},{4,12},{6,14},{8,16},{10,18},{12,20},{14,22},{1,9},{3... | collective-permute-start | bytes 3145736 | tf_op jit(solution)/shard_map/ppermute | solution.py:45
  251.2 11.4 %convolution_convert_fusion = bf16[256,4096]{1,0:T(8,128)(2,1)} fusion(bf16[2048,4096]{1,0:T(8,128)(2,1)} %param.10, bf16[32,8,16,128]{3,2,1,0:T(8,128)(2,1)S(1)} %bitcast.212), kind=kOutput, calls=%fused_computation.16 | convolution fusion | flops 4296015872 | bytes 19922944 | tf_op jit(solution)/shard_map/dot_general | solution.py:143
  262.7 9.6 %collective-permute-done.7 = bf16[2048,256]{1,0:T(8,128)(2,1)} collective-permute-done((bf16[2048,256]{1,0:T(8,128)(2,1)}, bf16[2048,256]{1,0:T(8,128)(2,1)}, u32[]{:S(2)}, u32[]{:S(2)}) %collective-permute-start.7) | collective-permute-done | bytes 1048608 | tf_op jit(solution)/shard_map/ppermute | solution.py:45
  272.3 4.7 %add_convert_fusion.2 = (bf16[2048,256]{1,0:T(8,128)(2,1)}, bf16[2048,256]{1,0:T(8,128)(2,1)}) fusion(bf16[2048,256]{1,0:T(8,128)(2,1)} %collective-permute-done.7, f32[2048,1024]{1,0:T(8,128)} %copy-done, s32[]{:T(128)S(6)} %select_n.81, bf16[2048,256]{1,0:T(8,128)(2,1)} %collective-permute-done.9, s32[]{:T(128)S(6)} %select_n.85), kind=kLoop, calls=%fused_computation.57 | loop fusion | flops 3145728 | bytes 8388616 | tf_op jit(solution)/shard_map/convert_element_type | solution.py:45
  286.3 5.1 %collective-permute-start.8 = (bf16[2048,256]{1,0:T(8,128)(2,1)}, bf16[2048,256]{1,0:T(8,128)(2,1)}, u32[]{:S(2)}, u32[]{:S(2)}) collective-permute-start(bf16[2048,256]{1,0:T(8,128)(2,1)} %get-tuple-element.21), channel_id=1, source_target_pairs={{0,8},{2,10},{4,12},{6,14},{8,16},{10,18},{12,20},{14,22},{16,24},... | collective-permute-start | bytes 3145736 | tf_op jit(solution)/shard_map/ppermute | solution.py:45
  291.4 3.1 add_convert_fusion
  297.7 2.8 copy.216
  300.4 2.6 copy.283
  311.9 19.1 %collective-permute-done.11 = bf16[2048,256]{1,0:T(8,128)(2,1)} collective-permute-done((bf16[2048,256]{1,0:T(8,128)(2,1)}, bf16[2048,256]{1,0:T(8,128)(2,1)}, u32[]{:S(2)}, u32[]{:S(2)}) %collective-permute-start.11) | collective-permute-done | bytes 1048608 | tf_op jit(solution)/shard_map/ppermute | solution.py:46
  330.9 3.8 %convert_add_fusion = f32[2048,256]{1,0:T(8,128)} fusion(bf16[2048,256]{1,0:T(8,128)(2,1)} %collective-permute-done.11, bf16[2048,256]{1,0:T(8,128)(2,1)} %collective-permute-done.8, f32[2048,1024]{1,0:T(8,128)} %copy-done, s32[]{:T(128)S(6)} %select_n.80), kind=kLoop, calls=%fused_computation.53 | loop fusion | flops 2097152 | bytes 6291460 | tf_op jit(solution)/shard_map/add | solution.py:47
  (138 shorter events, 70.3 us)
Async XLA Ops:
  7.2 12.5 %copy-start.21 = (bf16[256,2048]{1,0:T(8,128)(2,1)S(1)}, bf16[256,2048]{1,0:T(8,128)(2,1)}, u32[]{:S(2)}) copy-start(bf16[256,2048]{1,0:T(8,128)(2,1)} %param.6) | copy-start | bytes 3145732
  8.5 35.2 %all-to-all-start = ((s32[16,1,2]{2,1,0:T(1,128)}), s32[16,1,2]{2,1,0:T(1,128)S(1)}, u32[]{:S(2)}, u32[]{:S(2)}) async-start(s32[16,1,2]{2,1,0:T(1,128)} %broadcast_in_dim.96), calls=%async_computation | async-start | bytes 16384 | tf_op jit(solution)/shard_map/all_to_all | solution.py:61
  32.1 5.1 %copy-start.23 = (s32[2]{0:T(128)S(1)}, s32[2]{0:T(128)}, u32[]{:S(2)}) copy-start(s32[2]{0:T(128)} %param.9) | copy-start | bytes 28
  38.4 2.0 copy-start.6
  43.7 30.9 %all-to-all-start.1 = ((bf16[16,2,128,128]{3,2,1,0:T(8,128)(2,1)}), bf16[16,2,128,128]{3,2,1,0:T(8,128)(2,1)}, u32[]{:S(2)}, u32[]{:S(2)}) async-start(bf16[16,2,128,128]{3,2,1,0:T(8,128)(2,1)} %maximum_bitcast_fusion), calls=%async_computation.1 | async-start | bytes 2097152 | tf_op jit(solution)/shard_map/all_to_all | solution.py:69
  90.0 28.9 %all-to-all-start.2 = ((bf16[16,2,128,128]{3,2,1,0:T(8,128)(2,1)}), bf16[16,2,128,128]{3,2,1,0:T(8,128)(2,1)}, u32[]{:S(2)}, u32[]{:S(2)}) async-start(bf16[16,2,128,128]{3,2,1,0:T(8,128)(2,1)} %bitcast_dynamic-update-slice_fusion), calls=%async_computation.2 | async-start | bytes 2097152 | tf_op jit(solution)/shard_map/all_to_all | solution.py:76
  95.9 238.8 %reduce-scatter.2.cloned.1.call-start = ((), (), s32[]{:S(2)}) async-start(), calls=%async_computation.4 | async-start | bytes 3145728 | tf_op jit(solution)/shard_map/reduce_scatter | solution.py:145
  97.4 4.5 %copy-start.8 = (f32[2,16,128,128]{3,2,1,0:T(8,128)S(1)}, f32[2,16,128,128]{3,2,1,0:T(8,128)}, u32[]{:S(2)}) copy-start(f32[2,16,128,128]{3,2,1,0:T(8,128)} %get-tuple-element.66) | copy-start | bytes 6291460
  120.4 2.1 copy-start.15
  122.6 2.8 copy-start.11
  132.3 68.5 %collective-permute-start.3 = (bf16[256,2048]{1,0:T(8,128)(2,1)}, bf16[256,2048]{1,0:T(8,128)(2,1)}, u32[]{:S(2)}, u32[]{:S(2)}) collective-permute-start(bf16[256,2048]{1,0:T(8,128)(2,1)} %bitcast.194), channel_id=1, source_target_pairs={{0,6},{2,4},{4,2},{6,0},{8,14},{10,12},{12,10},{14,8},{16,22},{18,... | collective-permute-start | bytes 3145736 | tf_op jit(solution)/shard_map/ppermute | solution.py:153
  134.4 66.5 %collective-permute-start.2 = (bf16[256,2048]{1,0:T(8,128)(2,1)}, bf16[256,2048]{1,0:T(8,128)(2,1)}, u32[]{:S(2)}, u32[]{:S(2)}) collective-permute-start(bf16[256,2048]{1,0:T(8,128)(2,1)} %bitcast.194), channel_id=1, source_target_pairs={{0,4},{2,6},{4,0},{6,2},{8,12},{10,14},{12,8},{14,10},{16,20},{18,... | collective-permute-start | bytes 3145736 | tf_op jit(solution)/shard_map/ppermute | solution.py:153
  141.2 29.5 %collective-permute-start.5 = (bf16[256,1024]{0,1:T(8,128)(2,1)S(1)}, bf16[256,1024]{0,1:T(8,128)(2,1)S(1)}, u32[]{:S(2)}, u32[]{:S(2)}) collective-permute-start(bf16[256,1024]{0,1:T(8,128)(2,1)S(1)} %bitcast.225), channel_id=1, source_target_pairs={{0,6},{2,4},{4,2},{6,0},{8,14},{10,12},{12,10},{14,8},{16,22},{18,... | collective-permute-start | bytes 1572872 | tf_op jit(solution)/shard_map/ppermute | solution.py:100
  144.0 61.1 %collective-permute-start = (bf16[256,2048]{1,0:T(8,128)(2,1)}, bf16[256,2048]{1,0:T(8,128)(2,1)}, u32[]{:S(2)}, u32[]{:S(2)}) collective-permute-start(bf16[256,2048]{1,0:T(8,128)(2,1)} %bitcast.194), channel_id=1, source_target_pairs={{0,2},{2,0},{4,6},{6,4},{8,10},{10,8},{12,14},{14,12},{16,18},{18,... | collective-permute-start | bytes 3145736 | tf_op jit(solution)/shard_map/ppermute | solution.py:153
  144.7 56.2 %collective-permute-start.4 = (bf16[256,1024]{0,1:T(8,128)(2,1)}, bf16[256,1024]{0,1:T(8,128)(2,1)}, u32[]{:S(2)}, u32[]{:S(2)}) collective-permute-start(bf16[256,1024]{0,1:T(8,128)(2,1)} %bitcast.74), channel_id=1, source_target_pairs={{0,4},{2,6},{4,0},{6,2},{8,12},{10,14},{12,8},{14,10},{16,20},{18,... | collective-permute-start | bytes 1572872 | tf_op jit(solution)/shard_map/ppermute | solution.py:100
  171.6 33.5 %collective-permute-start.1 = (bf16[256,1024]{0,1:T(8,128)(2,1)}, bf16[256,1024]{0,1:T(8,128)(2,1)}, u32[]{:S(2)}, u32[]{:S(2)}) collective-permute-start(bf16[256,1024]{0,1:T(8,128)(2,1)} %bitcast.73), channel_id=1, source_target_pairs={{0,2},{2,0},{4,6},{6,4},{8,10},{10,8},{12,14},{14,12},{16,18},{18,... | collective-permute-start | bytes 1572872 | tf_op jit(solution)/shard_map/ppermute | solution.py:100
  172.2 32.9 %copy-start.20 = (bf16[256,4,1,256]{0,3,2,1:T(8,128)(2,1)S(1)}, bf16[256,4,1,256]{0,3,2,1:T(8,128)(2,1)}, u32[]{:S(2)}) copy-start(bf16[256,4,1,256]{0,3,2,1:T(8,128)(2,1)} %get-tuple-element.25) | copy-start | bytes 1572868
  209.3 3.2 copy-start
  214.1 28.6 %collective-permute-start.6 = (bf16[2048,256]{1,0:T(8,128)(2,1)}, bf16[2048,256]{1,0:T(8,128)(2,1)}, u32[]{:S(2)}, u32[]{:S(2)}) collective-permute-start(bf16[2048,256]{1,0:T(8,128)(2,1)} %get-tuple-element.23), channel_id=1, source_target_pairs={{0,8},{2,10},{4,12},{6,14},{1,9},{3,11},{5,13},{7,15}} | collective-permute-start | bytes 3145736 | tf_op jit(solution)/shard_map/ppermute | solution.py:45
  220.9 30.4 %copy-start.16 = (bf16[2,128,16,128]{3,2,1,0:T(8,128)(2,1)S(1)}, bf16[2,128,16,128]{3,2,1,0:T(8,128)(2,1)}, u32[]{:S(2)}) copy-start(bf16[2,128,16,128]{3,2,1,0:T(8,128)(2,1)} %copy.210) | copy-start | bytes 3145732
  220.9 41.8 %collective-permute-start.9 = (bf16[2048,256]{1,0:T(8,128)(2,1)}, bf16[2048,256]{1,0:T(8,128)(2,1)}, u32[]{:S(2)}, u32[]{:S(2)}) collective-permute-start(bf16[2048,256]{1,0:T(8,128)(2,1)} %get-tuple-element.24), channel_id=1, source_target_pairs={{24,16},{26,18},{28,20},{30,22},{25,17},{27,19},{29,21},{31,23}} | collective-permute-start | bytes 3145736 | tf_op jit(solution)/shard_map/ppermute | solution.py:46
  245.9 26.4 %collective-permute-start.7 = (bf16[2048,256]{1,0:T(8,128)(2,1)}, bf16[2048,256]{1,0:T(8,128)(2,1)}, u32[]{:S(2)}, u32[]{:S(2)}) collective-permute-start(bf16[2048,256]{1,0:T(8,128)(2,1)} %add_convert_fusion.3), channel_id=1, source_target_pairs={{0,8},{2,10},{4,12},{6,14},{8,16},{10,18},{12,20},{14,22},{1,9},{3... | collective-permute-start | bytes 3145736 | tf_op jit(solution)/shard_map/ppermute | solution.py:45
  262.7 15.9 %copy-start.4 = (bf16[32,8,16,128]{3,2,1,0:T(8,128)(2,1)S(1)}, bf16[32,8,16,128]{3,2,1,0:T(8,128)(2,1)}, u32[]{:S(2)}) copy-start(bf16[32,8,16,128]{3,2,1,0:T(8,128)(2,1)} %copy.237) | copy-start | bytes 3145732
  277.0 14.5 %collective-permute-start.10 = (bf16[2048,256]{1,0:T(8,128)(2,1)}, bf16[2048,256]{1,0:T(8,128)(2,1)}, u32[]{:S(2)}, u32[]{:S(2)}) collective-permute-start(bf16[2048,256]{1,0:T(8,128)(2,1)} %get-tuple-element.22), channel_id=1, source_target_pairs={{24,16},{26,18},{28,20},{30,22},{16,8},{18,10},{20,12},{22,14},{25... | collective-permute-start | bytes 3145736 | tf_op jit(solution)/shard_map/ppermute | solution.py:46
  280.5 2.2 copy-start.19
  286.3 9.5 %copy-start.3 = (bf16[2,16,128,128]{3,2,1,0:T(8,128)(2,1)S(1)}, bf16[2,16,128,128]{3,2,1,0:T(8,128)(2,1)}, u32[]{:S(2)}) copy-start(bf16[2,16,128,128]{3,2,1,0:T(8,128)(2,1)} %copy-done.2) | copy-start | bytes 3145732
  286.3 9.6 %copy-start.5 = (bf16[32,8,16,128]{3,2,1,0:T(8,128)(2,1)S(1)}, bf16[32,8,16,128]{3,2,1,0:T(8,128)(2,1)}, u32[]{:S(2)}) copy-start(bf16[32,8,16,128]{3,2,1,0:T(8,128)(2,1)} %copy.237) | copy-start | bytes 3145732
  286.3 25.6 %collective-permute-start.8 = (bf16[2048,256]{1,0:T(8,128)(2,1)}, bf16[2048,256]{1,0:T(8,128)(2,1)}, u32[]{:S(2)}, u32[]{:S(2)}) collective-permute-start(bf16[2048,256]{1,0:T(8,128)(2,1)} %get-tuple-element.21), channel_id=1, source_target_pairs={{0,8},{2,10},{4,12},{6,14},{8,16},{10,18},{12,20},{14,22},{16,24},... | collective-permute-start | bytes 3145736 | tf_op jit(solution)/shard_map/ppermute | solution.py:45
  294.6 36.4 %collective-permute-start.11 = (bf16[2048,256]{1,0:T(8,128)(2,1)}, bf16[2048,256]{1,0:T(8,128)(2,1)}, u32[]{:S(2)}, u32[]{:S(2)}) collective-permute-start(bf16[2048,256]{1,0:T(8,128)(2,1)} %add_convert_fusion), channel_id=1, source_target_pairs={{24,16},{26,18},{28,20},{30,22},{16,8},{18,10},{20,12},{22,14},{8,... | collective-permute-start | bytes 3145736 | tf_op jit(solution)/shard_map/ppermute | solution.py:46
  297.7 5.4 %copy-start.1 = (bf16[2,16,128,128]{3,2,1,0:T(8,128)(2,1)S(1)}, bf16[2,16,128,128]{3,2,1,0:T(8,128)(2,1)}, u32[]{:S(2)}) copy-start(bf16[2,16,128,128]{3,2,1,0:T(8,128)(2,1)} %get-tuple-element.70) | copy-start | bytes 3145732
  300.4 2.6 copy-start.10
  306.8 2.0 copy-start.9
  (9 other events, 12.9 us)
Sparse Core Ops, SparseCore 0:
  262.8 7.3 reduce-scatter.1

commit v3 on v1

--- a/solution.py
+++ b/solution.py
@@ -14,9 +14,11 @@
     while count % near:
         near += 1
     far = count // near
-    rows = [[r * near + c for c in range(near)] for r in range(far)]
-    columns = [[r * near + c for r in range(far)] for c in range(near)]
-    return near, far, rows, columns
+    return near, far
+
+
+def swapped(near, far, step):
+    return [(r * near + c, r * near + (c ^ step)) for r in range(far) for c in range(near)]
 
 
 def over_blocks(mask, states):
@@ -30,7 +32,9 @@
 
 def carried(states, grads, first_doc, last_doc):
     count, mine = (lax.axis_size("seq"), lax.axis_index("seq"))
-    ends = lax.all_gather(jnp.stack([first_doc, last_doc]), "seq")
+    ends = lax.all_to_all(
+        jnp.broadcast_to(jnp.stack([first_doc, last_doc]), (count, 2)), "seq", 0, 0
+    )
     firsts, lasts = (ends[:, 0], ends[:, 1])
     heads = states.shape[0]
     rows = heads * HD // count
@@ -57,10 +61,17 @@
     query_blocks = queries.reshape(block_count, BLK, heads_here, HD)
     key_blocks = key_rows.reshape(block_count, BLK, heads_here, HD)
     value_blocks = value_rows.reshape(block_count, BLK, heads_here, HD)
-    near, far, rows, columns = row_groups(lax.axis_size("seq"))
-    near_out = lax.all_to_all(
-        grad_output.reshape(tokens_here, far, near, -1), "seq", 2, 0, axis_index_groups=rows
-    ).reshape(near * tokens_here, -1)
+    near, far = row_groups(lax.axis_size("seq"))
+    seat = lax.axis_index("seq") % near
+    out_parts = grad_output.reshape(tokens_here, far, near, -1)
+
+    def out_part(place):
+        part = lax.dynamic_index_in_dim(out_parts, place, 2, keepdims=False)
+        return part.reshape(tokens_here, -1)
+
+    near_out = [out_part(seat)]
+    for step in range(1, near):
+        near_out.append(lax.ppermute(out_part(seat ^ step), "seq", swapped(near, far, step)))
     causal = jnp.tril(jnp.ones((BLK, BLK), dtype=bool))
     scores = (
         jnp.einsum("nthd,nshd->nhts", query_blocks, key_blocks, preferred_element_type=jnp.float32)
@@ -89,6 +100,7 @@
     own_grad = jnp.sum(
         jnp.where((doc_block == first_doc)[:, None, None, None], grad_states, 0.0), axis=0
     )
+    own_state, own_grad, near_out = lax.optimization_barrier((own_state, own_grad, near_out))
     carry_state, carry_grad = carried(own_state, own_grad, first_doc, last_doc)
     before = over_blocks(earlier, block_states)
     before = before + jnp.where(
@@ -111,18 +123,26 @@
         scatter_dimension=1,
         tiled=True,
     )
-    near_att = lax.all_gather(attended, "seq", axis_index_groups=rows, tiled=True)
-    weight_term = lax.dot_general(
-        near_att, near_out, (((0,), (0,)), ((), ())), preferred_element_type=jnp.float32
-    ).astype(jnp.bfloat16)
-    weight_parts = lax.all_to_all(
-        weight_term.reshape(width_here, far, -1),
-        "seq",
-        1,
-        0,
-        axis_index_groups=columns,
-    )
-    grad_weight = jnp.sum(weight_parts.astype(jnp.float32), axis=0)
+    columns = [[r * near + c for r in range(far)] for c in range(near)]
+    rows = [[r * near + c for c in range(near)] for r in range(far)]
+    near_out = jnp.stack(near_out)
+    near_out = jnp.concatenate(
+        [lax.dynamic_index_in_dim(near_out, seat ^ c, 0, keepdims=False) for c in range(near)]
+    )
+    half = width_here // 2
+    halves = []
+    for at in (0, half):
+        near_att = lax.all_gather(
+            attended[:, at : at + half], "seq", axis_index_groups=rows, tiled=True
+        )
+        weight_term = lax.dot_general(
+            near_att, near_out, (((0,), (0,)), ((), ())), preferred_element_type=jnp.float32
+        ).astype(jnp.bfloat16)
+        weight_parts = lax.all_to_all(
+            weight_term.reshape(half, far, -1), "seq", 1, 0, axis_index_groups=columns
+        )
+        halves.append(jnp.sum(weight_parts.astype(jnp.float32), axis=0))
+    grad_weight = jnp.concatenate(halves)
     grad_scores = (
         jnp.einsum("nthe,nshe->nhts", grad_blocks, value_blocks, preferred_element_type=jnp.float32)
         * factor

time: 322 us -> 294 us (0.913)
  blocking collectives: 61 us -> 0 us
  waiting for transfers between devices: 96 us -> 120 us
  starting transfers between devices: 18.3 us -> 34.4 us
  local copies, waits for them, and re-layouts: 52.8 us -> 45.4 us
    all_to_all x1 -> x0, blocking collectives: 36.7 us -> none  [body(): lax.all_to_all(grad_output.reshape(tokens_here, far, near, -1), 'seq', 2,...]
    unnamed x1 -> x0, blocking collectives: 24.3 us -> none
    all_to_all x1, waiting for transfers between devices: 0.01 us -> 21.5 us  [carried(): got = lax.all_to_all(both, 'seq', 0, 0).astype(jnp.float32)]
    all_gather x1 -> x2, waiting for transfers between devices: 26.4 us -> 47.6 us  [body(): lax.all_gather(attended[:, at:at + half], 'seq', axis_index_groups=rows,...]
    all_to_all x1 -> x3, waiting for transfers between devices: 54.9 us -> 36.9 us  [the longest x2 36.9 us: body(): lax.all_to_all(weight_term.reshape(half, far, -1), 'seq', 1, 0, axis_inde...]
    all_to_all x1 -> x3, starting transfers between devices: 4.84 us -> 16.7 us  [the longest x2 9.31 us: body(): lax.all_to_all(weight_term.reshape(half, far, -1), 'seq', 1, 0, axis_inde...]
    unnamed x65 -> x63, local copies, waits for them, and re-layouts: 33.7 us -> 27.3 us
    ppermute x0 -> x3, starting transfers between devices: none -> 4.46 us  [body(): lax.ppermute(out_part(seat ^ step), 'seq', swapped(near, far, step))]
  transfers between devices with their start and end apart: 5 -> 11, of which waited for: 3 -> 6; matrix products, arithmetic and copies ran while one was open for 19% -> 29% of each run, Pallas kernels for 0% -> 0%
where the time goes in v3:
time: 294 us; the launch traced here: 293 us
  waiting for transfers between devices  120 us (41%)
  matrix products  53.7 us (18%)
  local copies, waits for them, and re-layouts  45.4 us (15%)
  starting transfers between devices  34.4 us (12%)
  other arithmetic  23.7 us (8%)
  between operations  15.9 us (5%)
    all_gather x2, waiting for transfers between devices, body(): lax.all_gather(attended[:, at:at + half], 'seq', axis_index_groups=rows,...  47.6 us
    all_to_all x2, waiting for transfers between devices, body(): lax.all_to_all(weight_term.reshape(half, far, -1), 'seq', 1, 0, axis_inde...  36.9 us
    unnamed x63, local copies, waits for them, and re-layouts  27.3 us
    all_to_all x1, waiting for transfers between devices, carried(): got = lax.all_to_all(both, 'seq', 0, 0).astype(jnp.float32)  21.5 us
    all_to_all x1, waiting for transfers between devices, carried(): back = lax.all_to_all(summed, 'seq', 0, 0)  13.5 us
    dot_general x1, matrix products, body(): jnp.dot(attended, out_weight, preferred_element_type=jnp.float32)  11.9 us
    dot_general x2, matrix products, body(): lax.dot_general(near_att, near_out, (((0,), (0,)), ((), ())), preferred_e...  11.8 us
    dot_general x1, matrix products, body(): lax.dot_general(grad_output, out_weight, (((1,), (1,)), ((), ())), prefer...  10.9 us
  transfers between devices with their start and end apart: 11, of which 6 were waited for; matrix products, arithmetic and copies ran while one was open for 29% of the time, Pallas kernels for 0%

profile of v3, /device:TPU:0, one launch (start us, length us, event | category | flops | bytes accessed | tf_op | source)
XLA Modules:
  0.0 292.6 jit_solution(16329674698854793517)
XLA Ops:
  8.0 3.3 %copy.198 = bf16[256,4096]{0,1:T(8,128)(2,1)S(1)} copy(bf16[256,4096]{1,0:T(8,128)(2,1)} %param.11) | data formatting | bytes 4194304 | tf_op args[5]
  12.7 2.9 %collective-permute-start = (bf16[256,1024]{0,1:T(8,128)(2,1)}, bf16[256,1024]{0,1:T(8,128)(2,1)}, u32[]{:S(2)}, u32[]{:S(2)}) collective-permute-start(bf16[256,1024]{0,1:T(8,128)(2,1)} %bitcast.13), channel_id=1, source_target_pairs={{0,2},{2,0},{4,6},{6,4},{8,10},{10,8},{12,14},{14,12},{16,18},{18,... | collective-permute-start | bytes 1572872 | tf_op jit(solution)/shard_map/ppermute | solution.py:74
  17.8 7.3 %all-to-all-start = ((s32[16,1,2]{2,1,0:T(1,128)}), s32[16,1,2]{2,1,0:T(1,128)S(1)}, u32[]{:S(2)}, u32[]{:S(2)}) async-start(s32[16,1,2]{2,1,0:T(1,128)} %broadcast_in_dim.96), calls=%async_computation | async-start | bytes 16384 | tf_op jit(solution)/shard_map/all_to_all | solution.py:35
  25.7 10.9 %fusion.21 = bf16[32,8,16,128]{3,1,2,0:T(8,128)(2,1)S(1)} fusion(bf16[256,4096]{1,0:T(8,128)(2,1)} %param.11, bf16[2048,4096]{1,0:T(8,128)(2,1)} %param.10), kind=kOutput, calls=%fused_computation.58 | convolution fusion | flops 4295491584 | bytes 19922944 | tf_op jit(solution)/shard_map/dot_general | solution.py:84
  41.7 2.3 select_reduce_fusion
  43.9 2.0 select_reduce_fusion.1
  47.0 7.0 %all-to-all-start.1 = ((bf16[16,2,128,128]{3,2,1,0:T(8,128)(2,1)}), bf16[16,2,128,128]{3,2,1,0:T(8,128)(2,1)}, u32[]{:S(2)}, u32[]{:S(2)}) async-start(bf16[16,2,128,128]{3,2,1,0:T(8,128)(2,1)} %maximum_bitcast_fusion), calls=%async_computation.1 | async-start | bytes 2097152 | tf_op jit(solution)/shard_map/all_to_all | solution.py:43
  55.6 21.5 %all-to-all-done.1 = bf16[16,2,128,128]{3,2,1,0:T(8,128)(2,1)} async-done(((bf16[16,2,128,128]{3,2,1,0:T(8,128)(2,1)}), bf16[16,2,128,128]{3,2,1,0:T(8,128)(2,1)}, u32[]{:S(2)}, u32[]{:S(2)}) %all-to-all-start.1) | async-done | bytes 1048608 | tf_op jit(solution)/shard_map/all_to_all | solution.py:43
  77.1 5.4 %fusion.15 = (bf16[2,128,128]{2,1,0:T(8,128)(2,1)S(1)}, bf16[2,128,128]{2,1,0:T(8,128)(2,1)S(1)}, bf16[2,128,128]{2,1,0:T(8,128)(2,1)S(1)}, bf16[2,128,128]{2,1,...) fusion(bf16[16,2,128,128]{3,2,1,0:T(8,128)(2,1)} %all-to-all-do, ...), kind=kLoop, calls=%fused_computation.35 | loop fusion | flops 16777216 | bytes 2099200 | tf_op jit(solution)/shard_map/reduce_sum | solution.py:48
  92.7 6.0 %all-to-all-start.2 = ((bf16[16,2,128,128]{3,2,1,0:T(8,128)(2,1)}), bf16[16,2,128,128]{3,2,1,0:T(8,128)(2,1)}, u32[]{:S(2)}, u32[]{:S(2)}) async-start(bf16[16,2,128,128]{3,2,1,0:T(8,128)(2,1)} %bitcast_dynamic-update-slice_fusion), calls=%async_computation.2 | async-start | bytes 2097152 | tf_op jit(solution)/shard_map/all_to_all | solution.py:50
  99.7 4.3 %slice_multiply_fusion.3 = (f32[1,16,128,128]{3,2,1,0:T(8,128)}, f32[1,16,128,128]{3,2,1,0:T(8,128)}) fusion(f32[2,16,128,128]{3,2,1,0:T(8,128)} %get-tuple-element.90, f32[]{:T(128)} %bitcast.1, f32[]{:T(128)} %bitcast.2), kind=kLoop, calls=%fused_computation.69 | loop fusion | flops 524288 | bytes 4194312 | tf_op jit(solution)/shard_map/mul | solution.py:27
  105.9 2.2 fusion.29
  108.1 13.5 %all-to-all-done.2 = bf16[16,2,128,128]{3,2,1,0:T(8,128)(2,1)} async-done(((bf16[16,2,128,128]{3,2,1,0:T(8,128)(2,1)}), bf16[16,2,128,128]{3,2,1,0:T(8,128)(2,1)}, u32[]{:S(2)}, u32[]{:S(2)}) %all-to-all-start.2) | async-done | bytes 1048608 | tf_op jit(solution)/shard_map/all_to_all | solution.py:50
  127.0 1.9 fusion.20
  128.8 2.6 copy.216
  137.2 32.7 %all-gather.3.cloned.1.call-done = bf16[1024,1024]{1,0:T(8,128)(2,1)} async-done(((bf16[256,1024]{1,0:T(8,128)(2,1)}), bf16[1024,1024]{1,0:T(8,128)(2,1)}) %all-gather.3.cloned.1.call-update) | async-done | bytes 2097168 | tf_op jit(solution)/shard_map/all_gather | solution.py:135
  169.9 5.9 %convolution_convert_fusion.3 = bf16[1024,1024]{0,1:T(8,128)(2,1)} fusion(bf16[1024,1024]{1,0:T(8,128)(2,1)} %all-gather.3.cloned.1.call-done, bf16[256,1024]{0,1:T(8,128)(2,1)} %get-tuple-element.44, bf16[256,1024]{0,1:T(8,128)(2,1)} %get-tuple-element.45, bf16[256,1024]{0,1:T(8,128)(2,1)} %get-tuple-element.46, bf16[256,1024]{0,1:T(8,128)(2,1)} %get-tuple-element.43), kind=kOutput, calls=%fused_computation.56 | convolution fusion | flops 2156920832 | bytes 6291456 | tf_op jit(solution)/shard_map/dot_general | solution.py:138
  175.8 4.6 %all-to-all-start.3 = ((bf16[1,1024,4,256]{1,3,0,2:T(8,128)(2,1)}), bf16[1,1024,4,256]{1,3,0,2:T(8,128)(2,1)}, u32[]{:S(2)}, u32[]{:S(2)}) async-start(bf16[1,1024,4,256]{1,3,0,2:T(8,128)(2,1)} %bitcast.244), calls=%async_computation.4 | async-start | bytes 4194304 | tf_op jit(solution)/shard_map/all_to_all | solution.py:141
  180.4 11.9 %convolution_convert_fusion = bf16[256,4096]{1,0:T(8,128)(2,1)} fusion(bf16[2048,4096]{1,0:T(8,128)(2,1)} %param.10, bf16[32,8,16,128]{3,2,1,0:T(8,128)(2,1)} %bitcast.238), kind=kOutput, calls=%fused_computation.16 | convolution fusion | flops 4296015872 | bytes 19922944 | tf_op jit(solution)/shard_map/dot_general | solution.py:118
  192.3 14.9 %all-gather.5.cloned.1.call-done = bf16[1024,1024]{1,0:T(8,128)(2,1)} async-done(((bf16[256,1024]{1,0:T(8,128)(2,1)}), bf16[1024,1024]{1,0:T(8,128)(2,1)}) %all-gather.5.cloned.1.call-update) | async-done | bytes 2097168 | tf_op jit(solution)/shard_map/all_gather | solution.py:135
  207.2 5.9 %convolution_convert_fusion.2 = bf16[1024,1024]{0,1:T(8,128)(2,1)} fusion(bf16[1024,1024]{1,0:T(8,128)(2,1)} %all-gather.5.cloned.1.call-done, bf16[256,1024]{0,1:T(8,128)(2,1)} %get-tuple-element.44, bf16[256,1024]{0,1:T(8,128)(2,1)} %get-tuple-element.45, bf16[256,1024]{0,1:T(8,128)(2,1)} %get-tuple-element.46, bf16[256,1024]{0,1:T(8,128)(2,1)} %get-tuple-element.43), kind=kOutput, calls=%fused_computation.55 | convolution fusion | flops 2156920832 | bytes 6291456 | tf_op jit(solution)/shard_map/dot_general | solution.py:138
  213.2 15.6 %all-to-all-done.3 = bf16[1,1024,4,256]{1,3,0,2:T(8,128)(2,1)} async-done(((bf16[1,1024,4,256]{1,3,0,2:T(8,128)(2,1)}), bf16[1,1024,4,256]{1,3,0,2:T(8,128)(2,1)}, u32[]{:S(2)}, u32[]{:S(2)}) %all-to-all-start.3) | async-done | bytes 2097184 | tf_op jit(solution)/shard_map/all_to_all | solution.py:141
  228.8 4.7 %all-to-all-start.4 = ((bf16[1,1024,4,256]{1,3,0,2:T(8,128)(2,1)}), bf16[1,1024,4,256]{1,3,0,2:T(8,128)(2,1)}, u32[]{:S(2)}, u32[]{:S(2)}) async-start(bf16[1,1024,4,256]{1,3,0,2:T(8,128)(2,1)} %bitcast.243), calls=%async_computation.5 | async-start | bytes 4194304 | tf_op jit(solution)/shard_map/all_to_all | solution.py:141
  233.5 3.0 %slice_multiply_fusion.1 = (f32[1,16,128,128]{3,2,1,0:T(8,128)S(1)}, f32[1,16,128,128]{3,2,1,0:T(8,128)S(1)}) fusion(f32[2,16,128,128]{3,2,1,0:T(8,128)} %get-tuple-element.92, f32[]{:T(128)} %bitcast.71, f32[]{:T(128)} %bitcast.72), kind=kLoop, calls=%fused_computation.66 | loop fusion | flops 524288 | bytes 4194312 | tf_op jit(solution)/shard_map/mul | solution.py:27
  238.6 1.9 fusion.36
  240.5 2.2 fusion.33
  243.0 1.9 fusion.22
  244.9 1.9 copy.231
  250.6 2.1 copy.227
  257.8 2.1 convert_reduce_fusion.1
  259.9 21.2 %all-to-all-done.4 = bf16[1,1024,4,256]{1,3,0,2:T(8,128)(2,1)} async-done(((bf16[1,1024,4,256]{1,3,0,2:T(8,128)(2,1)}), bf16[1,1024,4,256]{1,3,0,2:T(8,128)(2,1)}, u32[]{:S(2)}, u32[]{:S(2)}) %all-to-all-start.4) | async-done | bytes 2097184 | tf_op jit(solution)/shard_map/all_to_all | solution.py:141
  281.1 2.1 convert_reduce_fusion
  (120 shorter events, 48.9 us)
Async XLA Ops:
  11.3 5.8 %copy-start.18 = (s32[2]{0:T(128)S(1)}, s32[2]{0:T(128)}, u32[]{:S(2)}) copy-start(s32[2]{0:T(128)} %param.9) | copy-start | bytes 28
  12.7 33.2 %collective-permute-start = (bf16[256,1024]{0,1:T(8,128)(2,1)}, bf16[256,1024]{0,1:T(8,128)(2,1)}, u32[]{:S(2)}, u32[]{:S(2)}) collective-permute-start(bf16[256,1024]{0,1:T(8,128)(2,1)} %bitcast.13), channel_id=1, source_target_pairs={{0,2},{2,0},{4,6},{6,4},{8,10},{10,8},{12,14},{14,12},{16,18},{18,... | collective-permute-start | bytes 1572872 | tf_op jit(solution)/shard_map/ppermute | solution.py:74
  15.6 30.3 %collective-permute-start.1 = (bf16[256,1024]{0,1:T(8,128)(2,1)}, bf16[256,1024]{0,1:T(8,128)(2,1)}, u32[]{:S(2)}, u32[]{:S(2)}) collective-permute-start(bf16[256,1024]{0,1:T(8,128)(2,1)} %bitcast.14), channel_id=1, source_target_pairs={{0,4},{2,6},{4,0},{6,2},{8,12},{10,14},{12,8},{14,10},{16,20},{18,... | collective-permute-start | bytes 1572872 | tf_op jit(solution)/shard_map/ppermute | solution.py:74
  17.2 28.8 %collective-permute-start.2 = (bf16[256,1024]{0,1:T(8,128)(2,1)}, bf16[256,1024]{0,1:T(8,128)(2,1)}, u32[]{:S(2)}, u32[]{:S(2)}) collective-permute-start(bf16[256,1024]{0,1:T(8,128)(2,1)} %bitcast.15), channel_id=1, source_target_pairs={{0,6},{2,4},{4,2},{6,0},{8,14},{10,12},{12,10},{14,8},{16,22},{18,... | collective-permute-start | bytes 1572872 | tf_op jit(solution)/shard_map/ppermute | solution.py:74
  17.8 29.2 %all-to-all-start = ((s32[16,1,2]{2,1,0:T(1,128)}), s32[16,1,2]{2,1,0:T(1,128)S(1)}, u32[]{:S(2)}, u32[]{:S(2)}) async-start(s32[16,1,2]{2,1,0:T(1,128)} %broadcast_in_dim.96), calls=%async_computation | async-start | bytes 16384 | tf_op jit(solution)/shard_map/all_to_all | solution.py:35
  36.7 2.0 copy-start.15
  36.9 2.0 copy-start.2
  38.6 1.2 copy-start.16
  38.6 1.5 copy-start.17
  39.8 1.8 copy-start.5
  47.0 30.1 %all-to-all-start.1 = ((bf16[16,2,128,128]{3,2,1,0:T(8,128)(2,1)}), bf16[16,2,128,128]{3,2,1,0:T(8,128)(2,1)}, u32[]{:S(2)}, u32[]{:S(2)}) async-start(bf16[16,2,128,128]{3,2,1,0:T(8,128)(2,1)} %maximum_bitcast_fusion), calls=%async_computation.1 | async-start | bytes 2097152 | tf_op jit(solution)/shard_map/all_to_all | solution.py:43
  92.7 28.9 %all-to-all-start.2 = ((bf16[16,2,128,128]{3,2,1,0:T(8,128)(2,1)}), bf16[16,2,128,128]{3,2,1,0:T(8,128)(2,1)}, u32[]{:S(2)}, u32[]{:S(2)}) async-start(bf16[16,2,128,128]{3,2,1,0:T(8,128)(2,1)} %bitcast_dynamic-update-slice_fusion), calls=%async_computation.2 | async-start | bytes 2097152 | tf_op jit(solution)/shard_map/all_to_all | solution.py:50
  98.7 71.2 %all-gather.3.cloned.1.call-start = ((), (), s32[]{:S(2)}) async-start(), calls=%async_computation.7 | async-start | bytes 2621440 | tf_op jit(solution)/shard_map/all_gather | solution.py:135
  104.8 1.1 copy-start.13
  123.1 1.5 copy-start.10
  123.1 1.9 copy-start.11
  125.0 2.0 copy-start.9
  125.4 1.0 copy-start
  134.0 73.2 %all-gather.5.cloned.1.call-start = ((), (), s32[]{:S(2)}) async-start(), calls=%async_computation.8 | async-start | bytes 2621440 | tf_op jit(solution)/shard_map/all_gather | solution.py:135
  175.8 53.0 %all-to-all-start.3 = ((bf16[1,1024,4,256]{1,3,0,2:T(8,128)(2,1)}), bf16[1,1024,4,256]{1,3,0,2:T(8,128)(2,1)}, u32[]{:S(2)}, u32[]{:S(2)}) async-start(bf16[1,1024,4,256]{1,3,0,2:T(8,128)(2,1)} %bitcast.244), calls=%async_computation.4 | async-start | bytes 4194304 | tf_op jit(solution)/shard_map/all_to_all | solution.py:141
  180.4 104.8 %reduce-scatter.2.cloned.1.call-start = ((), (), s32[]{:S(2)}) async-start(), calls=%async_computation.6 | async-start | bytes 3145728 | tf_op jit(solution)/shard_map/reduce_scatter | solution.py:120
  228.8 52.3 %all-to-all-start.4 = ((bf16[1,1024,4,256]{1,3,0,2:T(8,128)(2,1)}), bf16[1,1024,4,256]{1,3,0,2:T(8,128)(2,1)}, u32[]{:S(2)}, u32[]{:S(2)}) async-start(bf16[1,1024,4,256]{1,3,0,2:T(8,128)(2,1)} %bitcast.243), calls=%async_computation.5 | async-start | bytes 4194304 | tf_op jit(solution)/shard_map/all_to_all | solution.py:141
  233.5 3.1 %copy-start.3 = (bf16[32,8,16,128]{3,2,1,0:T(8,128)(2,1)S(1)}, bf16[32,8,16,128]{3,2,1,0:T(8,128)(2,1)}, u32[]{:S(2)}) copy-start(bf16[32,8,16,128]{3,2,1,0:T(8,128)(2,1)} %copy-done.2) | copy-start | bytes 3145732
  236.6 1.2 copy-start.6
  236.6 1.5 copy-start.14
  240.5 2.2 copy-start.12
  246.8 2.0 copy-start.8
  250.6 3.3 %copy-start.1 = (bf16[2,16,128,128]{3,2,1,0:T(8,128)(2,1)S(1)}, bf16[2,16,128,128]{3,2,1,0:T(8,128)(2,1)}, u32[]{:S(2)}) copy-start(bf16[2,16,128,128]{3,2,1,0:T(8,128)(2,1)} %copy-done) | copy-start | bytes 3145732
  250.6 3.3 %copy-start.4 = (bf16[32,8,16,128]{3,2,1,0:T(8,128)(2,1)S(1)}, bf16[32,8,16,128]{3,2,1,0:T(8,128)(2,1)}, u32[]{:S(2)}) copy-start(bf16[32,8,16,128]{3,2,1,0:T(8,128)(2,1)} %copy-done.2) | copy-start | bytes 3145732
  252.7 2.0 copy-start.7
Sparse Core Ops, SparseCore 0:
  134.2 35.6 all-gather.2
  171.9 35.2 all-gather.4
Sparse Core Ops, SparseCore 1:
  192.4 10.2 reduce-scatter.1

commit v4 on v3

--- a/solution.py
+++ b/solution.py
@@ -40,13 +40,14 @@
     rows = heads * HD // count
     both = jnp.stack([states, grads]).astype(jnp.bfloat16).reshape(2, count, rows, HD)
     both = jnp.moveaxis(both, 1, 0)
-    got = lax.all_to_all(both, "seq", 0, 0).astype(jnp.float32)
+    got = lax.all_to_all(both, "seq", 0, 0)
     place = jnp.arange(count)
     ahead = ((lasts[None, :] == firsts[:, None]) & (place[None, :] < place[:, None])).astype(jnp.float32)
     behind = ((firsts[None, :] == lasts[:, None]) & (place[None, :] > place[:, None])).astype(jnp.float32)
     masks = jnp.stack([ahead, behind])
-    summed = [jnp.sum(masks[:, j, :].T[:, :, None, None] * got, axis=0) for j in range(count)]
-    summed = jnp.stack(summed).astype(jnp.bfloat16)
+    summed = jnp.einsum(
+        "kji,ikrd->jkrd", masks.astype(jnp.bfloat16), got, preferred_element_type=jnp.float32
+    ).astype(jnp.bfloat16)
     back = lax.all_to_all(summed, "seq", 0, 0)
     back = jnp.moveaxis(back, 0, 1).reshape(2, heads, HD, HD).astype(jnp.float32)
     return back[0], back[1]
@@ -129,17 +130,17 @@
     near_out = jnp.concatenate(
         [lax.dynamic_index_in_dim(near_out, seat ^ c, 0, keepdims=False) for c in range(near)]
     )
-    half = width_here // 2
+    quarter = width_here // 4
     halves = []
-    for at in (0, half):
+    for at, wide in ((0, quarter), (quarter, quarter), (2 * quarter, 2 * quarter)):
         near_att = lax.all_gather(
-            attended[:, at : at + half], "seq", axis_index_groups=rows, tiled=True
+            attended[:, at : at + wide], "seq", axis_index_groups=rows, tiled=True
         )
         weight_term = lax.dot_general(
             near_att, near_out, (((0,), (0,)), ((), ())), preferred_element_type=jnp.float32
         ).astype(jnp.bfloat16)
         weight_parts = lax.all_to_all(
-            weight_term.reshape(half, far, -1), "seq", 1, 0, axis_index_groups=columns
+            weight_term.reshape(wide, far, -1), "seq", 1, 0, axis_index_groups=columns
         )
         halves.append(jnp.sum(weight_parts.astype(jnp.float32), axis=0))
     grad_weight = jnp.concatenate(halves)

time: 294 us -> 289 us (0.983)
  waiting for transfers between devices: 120 us -> 106 us
  other arithmetic: 23.7 us -> 18.9 us
  local copies, waits for them, and re-layouts: 45.4 us -> 50.1 us
  matrix products: 53.7 us -> 58 us
  starting transfers between devices: 34.4 us -> 38.6 us
    all_to_all x3 -> x4, waiting for transfers between devices: 58.4 us -> 44.2 us  [the longest x1 22.9 us: carried(): got = lax.all_to_all(both, 'seq', 0, 0)]
    another operation x1 -> x4, local copies, waits for them, and re-layouts: 0.63 us -> 9.93 us  [body(): lax.all_to_all(weight_term.reshape(wide, far, -1), 'seq', 1, 0, axis_inde...]
    unnamed x63 -> x54, local copies, waits for them, and re-layouts: 27.3 us -> 19.2 us
    reduce_sum x1 -> x0, other arithmetic: 5.43 us -> none  [carried(): jnp.sum(masks[:, j, :].T[:, :, None, None] * got, axis=0)]
    all_to_all x3 -> x4, starting transfers between devices: 16.3 us -> 20.5 us  [the longest x3 13.5 us: body(): lax.all_to_all(weight_term.reshape(wide, far, -1), 'seq', 1, 0, axis_inde...]
    dot_general x2 -> x3, matrix products: 11.8 us -> 14.2 us  [body(): lax.dot_general(near_att, near_out, (((0,), (0,)), ((), ())), preferred_e...]
    all_gather x2 -> x3, waiting for transfers between devices: 47.6 us -> 47.1 us  [body(): lax.all_gather(attended[:, at:at + wide], 'seq', axis_index_groups=rows,...]
  transfers between devices with their start and end apart: 11 -> 13, of which waited for: 6 -> 7; matrix products, arithmetic and copies ran while one was open for 29% -> 35% of each run, Pallas kernels for 0% -> 0%
where the time goes in v4:
time: 289 us; the launch traced here: 287 us
  waiting for transfers between devices  106 us (37%)
  matrix products  58 us (20%)
  local copies, waits for them, and re-layouts  50.1 us (17%)
  starting transfers between devices  38.6 us (13%)
  other arithmetic  18.9 us (7%)
  between operations  15.7 us (5%)
    all_gather x3, waiting for transfers between devices, body(): lax.all_gather(attended[:, at:at + wide], 'seq', axis_index_groups=rows,...  47.1 us
    all_to_all x1, waiting for transfers between devices, carried(): got = lax.all_to_all(both, 'seq', 0, 0)  22.9 us
    all_to_all x3, waiting for transfers between devices, body(): lax.all_to_all(weight_term.reshape(wide, far, -1), 'seq', 1, 0, axis_inde...  21.2 us
    unnamed x54, local copies, waits for them, and re-layouts  19.2 us
    dot_general x3, matrix products, body(): lax.dot_general(near_att, near_out, (((0,), (0,)), ((), ())), preferred_e...  14.2 us
    all_to_all x1, waiting for transfers between devices, carried(): back = lax.all_to_all(summed, 'seq', 0, 0)  13.7 us
    all_to_all x3, starting transfers between devices, body(): lax.all_to_all(weight_term.reshape(wide, far, -1), 'seq', 1, 0, axis_inde...  13.5 us
    dot_general x1, matrix products, body(): jnp.dot(attended, out_weight, preferred_element_type=jnp.float32)  11.9 us
  transfers between devices with their start and end apart: 13, of which 7 were waited for; matrix products, arithmetic and copies ran while one was open for 35% of the time, Pallas kernels for 0%

profile of v4, /device:TPU:0, one launch (start us, length us, event | category | flops | bytes accessed | tf_op | source)
XLA Modules:
  0.0 287.0 jit_solution(1933387715483789550)
XLA Ops:
  8.0 3.3 %copy.141 = bf16[256,4096]{0,1:T(8,128)(2,1)S(1)} copy(bf16[256,4096]{1,0:T(8,128)(2,1)} %param.11) | data formatting | bytes 4194304 | tf_op args[5]
  12.7 2.9 %collective-permute-start = (bf16[256,1024]{0,1:T(8,128)(2,1)}, bf16[256,1024]{0,1:T(8,128)(2,1)}, u32[]{:S(2)}, u32[]{:S(2)}) collective-permute-start(bf16[256,1024]{0,1:T(8,128)(2,1)} %bitcast.8), channel_id=1, source_target_pairs={{0,2},{2,0},{4,6},{6,4},{8,10},{10,8},{12,14},{14,12},{16,18},{18,... | collective-permute-start | bytes 1572872 | tf_op jit(solution)/shard_map/ppermute | solution.py:75
  17.8 7.3 %all-to-all-start.1 = ((s32[16,1,2]{2,1,0:T(1,128)}), s32[16,1,2]{2,1,0:T(1,128)S(1)}, u32[]{:S(2)}, u32[]{:S(2)}) async-start(s32[16,1,2]{2,1,0:T(1,128)} %broadcast_in_dim.81), calls=%async_computation.1 | async-start | bytes 16384 | tf_op jit(solution)/shard_map/all_to_all | solution.py:35
  25.7 10.9 %fusion.5 = bf16[32,8,16,128]{3,1,2,0:T(8,128)(2,1)S(1)} fusion(bf16[256,4096]{1,0:T(8,128)(2,1)} %param.11, bf16[2048,4096]{1,0:T(8,128)(2,1)} %param.10), kind=kOutput, calls=%fused_computation.29 | convolution fusion | flops 4295491584 | bytes 19922944 | tf_op jit(solution)/shard_map/dot_general | solution.py:85
  41.7 2.3 select_reduce_fusion
  43.9 2.0 select_reduce_fusion.1
  47.1 7.0 %all-to-all-start = ((bf16[16,2,128,128]{3,2,1,0:T(8,128)(2,1)}), bf16[16,2,128,128]{3,2,1,0:T(8,128)(2,1)}, u32[]{:S(2)}, u32[]{:S(2)}) async-start(bf16[16,2,128,128]{3,2,1,0:T(8,128)(2,1)} %copy.142), calls=%async_computation | async-start | bytes 2097152 | tf_op jit(solution)/shard_map/all_to_all | solution.py:43
  54.2 22.9 %all-to-all-done = bf16[16,2,128,128]{3,2,1,0:T(8,128)(2,1)} async-done(((bf16[16,2,128,128]{3,2,1,0:T(8,128)(2,1)}), bf16[16,2,128,128]{3,2,1,0:T(8,128)(2,1)}, u32[]{:S(2)}, u32[]{:S(2)}) %all-to-all-start) | async-done | bytes 1048608 | tf_op jit(solution)/shard_map/all_to_all | solution.py:43
  80.4 6.0 %all-to-all-start.2 = ((bf16[16,2,128,128]{3,2,1,0:T(8,128)(2,1)}), bf16[16,2,128,128]{3,2,1,0:T(8,128)(2,1)}, u32[]{:S(2)}, u32[]{:S(2)}) async-start(bf16[16,2,128,128]{3,2,1,0:T(8,128)(2,1)} %copy.145), calls=%async_computation.2 | async-start | bytes 2097152 | tf_op jit(solution)/shard_map/all_to_all | solution.py:51
  87.3 4.2 %slice_multiply_fusion.3 = (f32[1,16,128,128]{3,2,1,0:T(8,128)}, f32[1,16,128,128]{3,2,1,0:T(8,128)}) fusion(f32[2,16,128,128]{3,2,1,0:T(8,128)} %get-tuple-element.58, f32[]{:T(128)} %bitcast.1, f32[]{:T(128)} %bitcast.2), kind=kLoop, calls=%fused_computation.41 | loop fusion | flops 524288 | bytes 4194312 | tf_op jit(solution)/shard_map/mul | solution.py:27
  93.4 2.2 fusion.15
  95.6 13.7 %all-to-all-done.2 = bf16[16,2,128,128]{3,2,1,0:T(8,128)(2,1)} async-done(((bf16[16,2,128,128]{3,2,1,0:T(8,128)(2,1)}), bf16[16,2,128,128]{3,2,1,0:T(8,128)(2,1)}, u32[]{:S(2)}, u32[]{:S(2)}) %all-to-all-start.2) | async-done | bytes 1048608 | tf_op jit(solution)/shard_map/all_to_all | solution.py:51
  116.5 2.6 copy.148
  127.8 21.9 %all-gather.4.cloned.1.call-done = bf16[1024,512]{1,0:T(8,128)(2,1)} async-done(((bf16[256,512]{1,0:T(8,128)(2,1)}), bf16[1024,512]{1,0:T(8,128)(2,1)}) %all-gather.4.cloned.1.call-update) | async-done | bytes 1048592 | tf_op jit(solution)/shard_map/all_gather | solution.py:136
  149.7 4.1 %convolution_convert_fusion.5 = bf16[512,1024]{1,0:T(8,128)(2,1)} fusion(bf16[1024,512]{1,0:T(8,128)(2,1)} %all-gather.4.cloned.1.call-done, bf16[256,1024]{0,1:T(8,128)(2,1)} %get-tuple-element.28, bf16[256,1024]{0,1:T(8,128)(2,1)} %get-tuple-element.29, bf16[256,1024]{0,1:T(8,128)(2,1)} %get-tuple-element.30, bf16[256,1024]{0,1:T(8,128)(2,1)} %get-tuple-element.27), kind=kOutput, calls=%fused_computation.28 | convolution fusion | flops 1082654720 | bytes 4194304 | tf_op jit(solution)/shard_map/dot_general | solution.py:139
  153.8 2.6 broadcast_in_dim_reshape.9
  156.4 2.3 copy.164
  158.7 4.6 %all-to-all-start.3 = ((bf16[1,512,4,256]{3,1,0,2:T(8,128)(2,1)}), bf16[1,512,4,256]{3,1,0,2:T(8,128)(2,1)}, u32[]{:S(2)}, u32[]{:S(2)}) async-start(bf16[1,512,4,256]{3,1,0,2:T(8,128)(2,1)} %copy.164), calls=%async_computation.4 | async-start | bytes 2097152 | tf_op jit(solution)/shard_map/all_to_all | solution.py:142
  163.3 15.0 %all-gather.6.cloned.1.call-done = bf16[1024,512]{1,0:T(8,128)(2,1)} async-done(((bf16[256,512]{1,0:T(8,128)(2,1)}), bf16[1024,512]{1,0:T(8,128)(2,1)}) %all-gather.6.cloned.1.call-update) | async-done | bytes 1048592 | tf_op jit(solution)/shard_map/all_gather | solution.py:136
  178.3 4.1 %convolution_convert_fusion.4 = bf16[512,1024]{1,0:T(8,128)(2,1)} fusion(bf16[1024,512]{1,0:T(8,128)(2,1)} %all-gather.6.cloned.1.call-done, bf16[256,1024]{0,1:T(8,128)(2,1)} %get-tuple-element.28, bf16[256,1024]{0,1:T(8,128)(2,1)} %get-tuple-element.29, bf16[256,1024]{0,1:T(8,128)(2,1)} %get-tuple-element.30, bf16[256,1024]{0,1:T(8,128)(2,1)} %get-tuple-element.27), kind=kOutput, calls=%fused_computation.27 | convolution fusion | flops 1082654720 | bytes 4194304 | tf_op jit(solution)/shard_map/dot_general | solution.py:139
  182.4 2.6 broadcast_in_dim_reshape.10
  185.0 2.3 copy.165
  189.2 4.2 %all-to-all-start.4 = ((bf16[1,512,4,256]{3,1,0,2:T(8,128)(2,1)}), bf16[1,512,4,256]{3,1,0,2:T(8,128)(2,1)}, u32[]{:S(2)}, u32[]{:S(2)}) async-start(bf16[1,512,4,256]{3,1,0,2:T(8,128)(2,1)} %copy.165), calls=%async_computation.5 | async-start | bytes 2097152 | tf_op jit(solution)/shard_map/all_to_all | solution.py:142
  193.5 11.9 %convolution_convert_fusion = bf16[256,4096]{1,0:T(8,128)(2,1)} fusion(bf16[2048,4096]{1,0:T(8,128)(2,1)} %param.10, bf16[32,8,16,128]{3,2,1,0:T(8,128)(2,1)} %bitcast.144), kind=kOutput, calls=%fused_computation | convolution fusion | flops 4296015872 | bytes 19922944 | tf_op jit(solution)/shard_map/dot_general | solution.py:119
  205.4 10.2 %all-gather.8.cloned.1.call-done = bf16[1024,1024]{1,0:T(8,128)(2,1)} async-done(((bf16[256,1024]{1,0:T(8,128)(2,1)}), bf16[1024,1024]{1,0:T(8,128)(2,1)}) %all-gather.8.cloned.1.call-update) | async-done | bytes 2097168 | tf_op jit(solution)/shard_map/all_gather | solution.py:136
  215.6 6.0 %convolution_convert_fusion.2 = bf16[1024,1024]{0,1:T(8,128)(2,1)} fusion(bf16[1024,1024]{1,0:T(8,128)(2,1)} %all-gather.8.cloned.1.call-done, bf16[256,1024]{0,1:T(8,128)(2,1)} %get-tuple-element.28, bf16[256,1024]{0,1:T(8,128)(2,1)} %get-tuple-element.29, bf16[256,1024]{0,1:T(8,128)(2,1)} %get-tuple-element.30, bf16[256,1024]{0,1:T(8,128)(2,1)} %get-tuple-element.27), kind=kOutput, calls=%fused_computation.24 | convolution fusion | flops 2156920832 | bytes 6291456 | tf_op jit(solution)/shard_map/dot_general | solution.py:139
  221.6 4.7 %all-to-all-start.5 = ((bf16[1,1024,4,256]{1,3,0,2:T(8,128)(2,1)}), bf16[1,1024,4,256]{1,3,0,2:T(8,128)(2,1)}, u32[]{:S(2)}, u32[]{:S(2)}) async-start(bf16[1,1024,4,256]{1,3,0,2:T(8,128)(2,1)} %bitcast.150), calls=%async_computation.6 | async-start | bytes 4194304 | tf_op jit(solution)/shard_map/all_to_all | solution.py:142
  226.3 3.0 %slice_multiply_fusion.1 = (f32[1,16,128,128]{3,2,1,0:T(8,128)S(1)}, f32[1,16,128,128]{3,2,1,0:T(8,128)S(1)}) fusion(f32[2,16,128,128]{3,2,1,0:T(8,128)} %get-tuple-element.60, f32[]{:T(128)} %bitcast.26, f32[]{:T(128)} %bitcast.27), kind=kLoop, calls=%fused_computation.38 | loop fusion | flops 524288 | bytes 4194312 | tf_op jit(solution)/shard_map/mul | solution.py:27
  233.1 2.2 fusion.19
  243.3 2.1 copy.159
  255.2 19.4 %all-to-all-done.5 = bf16[1,1024,4,256]{1,3,0,2:T(8,128)(2,1)} async-done(((bf16[1,1024,4,256]{1,3,0,2:T(8,128)(2,1)}), bf16[1,1024,4,256]{1,3,0,2:T(8,128)(2,1)}, u32[]{:S(2)}, u32[]{:S(2)}) %all-to-all-start.5) | async-done | bytes 2097184 | tf_op jit(solution)/shard_map/all_to_all | solution.py:142
  274.7 2.1 convert_reduce_fusion
  (108 shorter events, 58.5 us)
Async XLA Ops:
  11.3 5.8 %copy-start.21 = (s32[2]{0:T(128)S(1)}, s32[2]{0:T(128)}, u32[]{:S(2)}) copy-start(s32[2]{0:T(128)} %param.9) | copy-start | bytes 28
  12.7 33.2 %collective-permute-start = (bf16[256,1024]{0,1:T(8,128)(2,1)}, bf16[256,1024]{0,1:T(8,128)(2,1)}, u32[]{:S(2)}, u32[]{:S(2)}) collective-permute-start(bf16[256,1024]{0,1:T(8,128)(2,1)} %bitcast.8), channel_id=1, source_target_pairs={{0,2},{2,0},{4,6},{6,4},{8,10},{10,8},{12,14},{14,12},{16,18},{18,... | collective-permute-start | bytes 1572872 | tf_op jit(solution)/shard_map/ppermute | solution.py:75
  15.6 30.3 %collective-permute-start.1 = (bf16[256,1024]{0,1:T(8,128)(2,1)}, bf16[256,1024]{0,1:T(8,128)(2,1)}, u32[]{:S(2)}, u32[]{:S(2)}) collective-permute-start(bf16[256,1024]{0,1:T(8,128)(2,1)} %bitcast.9), channel_id=1, source_target_pairs={{0,4},{2,6},{4,0},{6,2},{8,12},{10,14},{12,8},{14,10},{16,20},{18,... | collective-permute-start | bytes 1572872 | tf_op jit(solution)/shard_map/ppermute | solution.py:75
  17.2 28.8 %collective-permute-start.2 = (bf16[256,1024]{0,1:T(8,128)(2,1)}, bf16[256,1024]{0,1:T(8,128)(2,1)}, u32[]{:S(2)}, u32[]{:S(2)}) collective-permute-start(bf16[256,1024]{0,1:T(8,128)(2,1)} %bitcast.10), channel_id=1, source_target_pairs={{0,6},{2,4},{4,2},{6,0},{8,14},{10,12},{12,10},{14,8},{16,22},{18,... | collective-permute-start | bytes 1572872 | tf_op jit(solution)/shard_map/ppermute | solution.py:75
  17.8 29.3 %all-to-all-start.1 = ((s32[16,1,2]{2,1,0:T(1,128)}), s32[16,1,2]{2,1,0:T(1,128)S(1)}, u32[]{:S(2)}, u32[]{:S(2)}) async-start(s32[16,1,2]{2,1,0:T(1,128)} %broadcast_in_dim.81), calls=%async_computation.1 | async-start | bytes 16384 | tf_op jit(solution)/shard_map/all_to_all | solution.py:35
  36.6 2.0 copy-start.18
  36.9 2.0 copy-start.2
  38.6 1.2 copy-start.19
  38.6 1.5 copy-start.20
  39.8 1.8 copy-start.5
  47.1 30.1 %all-to-all-start = ((bf16[16,2,128,128]{3,2,1,0:T(8,128)(2,1)}), bf16[16,2,128,128]{3,2,1,0:T(8,128)(2,1)}, u32[]{:S(2)}, u32[]{:S(2)}) async-start(bf16[16,2,128,128]{3,2,1,0:T(8,128)(2,1)} %copy.142), calls=%async_computation | async-start | bytes 2097152 | tf_op jit(solution)/shard_map/all_to_all | solution.py:43
  80.4 28.9 %all-to-all-start.2 = ((bf16[16,2,128,128]{3,2,1,0:T(8,128)(2,1)}), bf16[16,2,128,128]{3,2,1,0:T(8,128)(2,1)}, u32[]{:S(2)}, u32[]{:S(2)}) async-start(bf16[16,2,128,128]{3,2,1,0:T(8,128)(2,1)} %copy.145), calls=%async_computation.2 | async-start | bytes 2097152 | tf_op jit(solution)/shard_map/all_to_all | solution.py:51
  86.4 63.3 %all-gather.4.cloned.1.call-start = ((), (), s32[]{:S(2)}) async-start(), calls=%async_computation.8 | async-start | bytes 1310720 | tf_op jit(solution)/shard_map/all_gather | solution.py:136
  110.8 1.5 copy-start.10
  110.8 1.9 copy-start.11
  112.7 2.0 copy-start.9
  122.5 55.8 %all-gather.6.cloned.1.call-start = ((), (), s32[]{:S(2)}) async-start(), calls=%async_computation.9 | async-start | bytes 1310720 | tf_op jit(solution)/shard_map/all_gather | solution.py:136
  123.2 92.4 %all-gather.8.cloned.1.call-start = ((), (), s32[]{:S(2)}) async-start(), calls=%async_computation.10 | async-start | bytes 2621440 | tf_op jit(solution)/shard_map/all_gather | solution.py:136
  125.1 1.8 copy-start.14
  158.7 30.4 %all-to-all-start.3 = ((bf16[1,512,4,256]{3,1,0,2:T(8,128)(2,1)}), bf16[1,512,4,256]{3,1,0,2:T(8,128)(2,1)}, u32[]{:S(2)}, u32[]{:S(2)}) async-start(bf16[1,512,4,256]{3,1,0,2:T(8,128)(2,1)} %copy.164), calls=%async_computation.4 | async-start | bytes 2097152 | tf_op jit(solution)/shard_map/all_to_all | solution.py:142
  189.2 32.4 %all-to-all-start.4 = ((bf16[1,512,4,256]{3,1,0,2:T(8,128)(2,1)}), bf16[1,512,4,256]{3,1,0,2:T(8,128)(2,1)}, u32[]{:S(2)}, u32[]{:S(2)}) async-start(bf16[1,512,4,256]{3,1,0,2:T(8,128)(2,1)} %copy.165), calls=%async_computation.5 | async-start | bytes 2097152 | tf_op jit(solution)/shard_map/all_to_all | solution.py:142
  193.4 86.4 %reduce-scatter.2.cloned.1.call-start = ((), (), s32[]{:S(2)}) async-start(), calls=%async_computation.7 | async-start | bytes 3145728 | tf_op jit(solution)/shard_map/reduce_scatter | solution.py:121
  221.6 53.1 %all-to-all-start.5 = ((bf16[1,1024,4,256]{1,3,0,2:T(8,128)(2,1)}), bf16[1,1024,4,256]{1,3,0,2:T(8,128)(2,1)}, u32[]{:S(2)}, u32[]{:S(2)}) async-start(bf16[1,1024,4,256]{1,3,0,2:T(8,128)(2,1)} %bitcast.150), calls=%async_computation.6 | async-start | bytes 4194304 | tf_op jit(solution)/shard_map/all_to_all | solution.py:142
  226.3 3.0 %copy-start.3 = (bf16[32,8,16,128]{3,2,1,0:T(8,128)(2,1)S(1)}, bf16[32,8,16,128]{3,2,1,0:T(8,128)(2,1)}, u32[]{:S(2)}) copy-start(bf16[32,8,16,128]{3,2,1,0:T(8,128)(2,1)} %copy-done.2) | copy-start | bytes 3145732
  229.3 1.2 copy-start.6
  229.3 1.5 copy-start.16
  233.1 2.2 copy-start.12
  239.5 2.0 copy-start.8
  243.3 3.3 %copy-start.1 = (bf16[2,16,128,128]{3,2,1,0:T(8,128)(2,1)S(1)}, bf16[2,16,128,128]{3,2,1,0:T(8,128)(2,1)}, u32[]{:S(2)}) copy-start(bf16[2,16,128,128]{3,2,1,0:T(8,128)(2,1)} %copy-done) | copy-start | bytes 3145732
  243.3 3.3 %copy-start.4 = (bf16[32,8,16,128]{3,2,1,0:T(8,128)(2,1)S(1)}, bf16[32,8,16,128]{3,2,1,0:T(8,128)(2,1)}, u32[]{:S(2)}) copy-start(bf16[32,8,16,128]{3,2,1,0:T(8,128)(2,1)} %copy-done.2) | copy-start | bytes 3145732
  245.4 2.0 copy-start.7
  274.7 2.1 copy-start.17
  (3 other events, 2.9 us)
Sparse Core Ops, SparseCore 0:
  122.6 27.0 all-gather.3
  151.6 26.6 all-gather.5
  180.3 35.2 all-gather.7
Sparse Core Ops, SparseCore 1:
  205.5 9.9 reduce-scatter.1

commit v5 on v4

--- a/solution.py
+++ b/solution.py
@@ -32,15 +32,15 @@
 
 def carried(states, grads, first_doc, last_doc):
     count, mine = (lax.axis_size("seq"), lax.axis_index("seq"))
-    ends = lax.all_to_all(
-        jnp.broadcast_to(jnp.stack([first_doc, last_doc]), (count, 2)), "seq", 0, 0
-    )
-    firsts, lasts = (ends[:, 0], ends[:, 1])
     heads = states.shape[0]
     rows = heads * HD // count
     both = jnp.stack([states, grads]).astype(jnp.bfloat16).reshape(2, count, rows, HD)
     both = jnp.moveaxis(both, 1, 0)
-    got = lax.all_to_all(both, "seq", 0, 0)
+    ends = jnp.stack([first_doc, last_doc]).astype(jnp.bfloat16)
+    ends = jnp.broadcast_to(ends[None, :, None, None], (count, 2, 16, HD))
+    got = lax.all_to_all(jnp.concatenate([both, ends], axis=2), "seq", 0, 0)
+    firsts, lasts = (got[:, 0, rows, 0], got[:, 1, rows, 0])
+    got = got[:, :, :rows]
     place = jnp.arange(count)
     ahead = ((lasts[None, :] == firsts[:, None]) & (place[None, :] < place[:, None])).astype(jnp.float32)
     behind = ((firsts[None, :] == lasts[:, None]) & (place[None, :] > place[:, None])).astype(jnp.float32)

time: 289 us -> 284 us (0.983)
  blocking collectives: 0 us -> 34.6 us
  waiting for transfers between devices: 106 us -> 85.2 us
  starting transfers between devices: 38.6 us -> 22.7 us
    all_to_all x0 -> x1, blocking collectives: none -> 34.6 us  [carried(): got = lax.all_to_all(jnp.concatenate([both, ends], axis=2), 'seq', 0, 0)]
    all_to_all x2 -> x0, waiting for transfers between devices: 22.9 us -> none  [the longest x1 22.9 us: carried(): got = lax.all_to_all(both, 'seq', 0, 0)]
    all_to_all x2 -> x0, starting transfers between devices: 14.3 us -> none  [the longest x1 7.34 us: carried(): lax.all_to_all(jnp.broadcast_to(jnp.stack([first_doc, last_doc]), (count,...]
  transfers between devices with their start and end apart: 13 -> 11, of which waited for: 7 -> 7; matrix products, arithmetic and copies ran while one was open for 35% -> 35% of each run, Pallas kernels for 0% -> 0%
where the time goes in v5:
time: 284 us; the launch traced here: 283 us
  waiting for transfers between devices  85.2 us (30%)
  matrix products  56.8 us (20%)
  local copies, waits for them, and re-layouts  49 us (17%)
  blocking collectives  34.6 us (12%)
  starting transfers between devices  22.7 us (8%)
  other arithmetic  19.2 us (7%)
  between operations  15.7 us (6%)
    all_gather x3, waiting for transfers between devices, body(): lax.all_gather(attended[:, at:at + wide], 'seq', axis_index_groups=rows,...  46.9 us
    all_to_all x1, blocking collectives, carried(): got = lax.all_to_all(jnp.concatenate([both, ends], axis=2), 'seq', 0, 0)  34.6 us
    all_to_all x3, waiting for transfers between devices, body(): lax.all_to_all(weight_term.reshape(wide, far, -1), 'seq', 1, 0, axis_inde...  21.2 us
    unnamed x54, local copies, waits for them, and re-layouts  19.2 us
    dot_general x3, matrix products, body(): lax.dot_general(near_att, near_out, (((0,), (0,)), ((), ())), preferred_e...  14.2 us
    all_to_all x1, waiting for transfers between devices, carried(): back = lax.all_to_all(summed, 'seq', 0, 0)  13.7 us
    all_to_all x3, starting transfers between devices, body(): lax.all_to_all(weight_term.reshape(wide, far, -1), 'seq', 1, 0, axis_inde...  13.5 us
    dot_general x1, matrix products, body(): jnp.dot(attended, out_weight, preferred_element_type=jnp.float32)  11.9 us
  transfers between devices with their start and end apart: 11, of which 7 were waited for; matrix products, arithmetic and copies ran while one was open for 35% of the time, Pallas kernels for 0%

profile of v5, /device:TPU:0, one launch (start us, length us, event | category | flops | bytes accessed | tf_op | source)
XLA Modules:
  0.0 283.0 jit_solution(4607635748574060425)
XLA Ops:
  8.0 3.3 %copy.140 = bf16[256,4096]{0,1:T(8,128)(2,1)S(1)} copy(bf16[256,4096]{1,0:T(8,128)(2,1)} %param.11) | data formatting | bytes 4194304 | tf_op args[5]
  12.7 2.9 %collective-permute-start = (bf16[256,1024]{0,1:T(8,128)(2,1)}, bf16[256,1024]{0,1:T(8,128)(2,1)}, u32[]{:S(2)}, u32[]{:S(2)}) collective-permute-start(bf16[256,1024]{0,1:T(8,128)(2,1)} %bitcast.8), channel_id=1, source_target_pairs={{0,2},{2,0},{4,6},{6,4},{8,10},{10,8},{12,14},{14,12},{16,18},{18,... | collective-permute-start | bytes 1572872 | tf_op jit(solution)/shard_map/ppermute | solution.py:75
  17.8 10.9 %fusion.5 = bf16[32,8,16,128]{3,1,2,0:T(8,128)(2,1)S(1)} fusion(bf16[256,4096]{1,0:T(8,128)(2,1)} %param.11, bf16[2048,4096]{1,0:T(8,128)(2,1)} %param.10), kind=kOutput, calls=%fused_computation.29 | convolution fusion | flops 4295491584 | bytes 19922944 | tf_op jit(solution)/shard_map/dot_general | solution.py:85
  33.7 2.2 select_reduce_fusion
  35.9 2.0 select_reduce_fusion.1
  37.9 2.7 collective-permute-done.1
  41.0 34.6 %all_to_all.37 = bf16[16,2,144,128]{3,2,1,0:T(8,128)(2,1)S(1)} all-to-all(bf16[16,2,144,128]{3,2,1,0:T(8,128)(2,1)S(1)} %copy.141), channel_id=1, replica_groups=mesh['seq'=16,'head'=2] {'seq'}, dimensions={0} | all-to-all | bytes 2359296 | tf_op jit(solution)/shard_map/all_to_all | solution.py:41
  78.0 4.3 %all-to-all-start.1 = ((bf16[16,2,128,128]{3,2,1,0:T(8,128)(2,1)}), bf16[16,2,128,128]{3,2,1,0:T(8,128)(2,1)}, u32[]{:S(2)}, u32[]{:S(2)}) async-start(bf16[16,2,128,128]{3,2,1,0:T(8,128)(2,1)} %copy.143), calls=%async_computation.1 | async-start | bytes 2097152 | tf_op jit(solution)/shard_map/all_to_all | solution.py:51
  83.3 4.5 %slice_multiply_fusion.3 = (f32[1,16,128,128]{3,2,1,0:T(8,128)}, f32[1,16,128,128]{3,2,1,0:T(8,128)}) fusion(f32[2,16,128,128]{3,2,1,0:T(8,128)} %get-tuple-element.58, f32[]{:T(128)} %bitcast.1, f32[]{:T(128)} %bitcast.2), kind=kLoop, calls=%fused_computation.42 | loop fusion | flops 524288 | bytes 4194312 | tf_op jit(solution)/shard_map/mul | solution.py:27
  89.6 2.2 fusion.15
  91.8 13.7 %all-to-all-done.1 = bf16[16,2,128,128]{3,2,1,0:T(8,128)(2,1)} async-done(((bf16[16,2,128,128]{3,2,1,0:T(8,128)(2,1)}), bf16[16,2,128,128]{3,2,1,0:T(8,128)(2,1)}, u32[]{:S(2)}, u32[]{:S(2)}) %all-to-all-start.1) | async-done | bytes 1048608 | tf_op jit(solution)/shard_map/all_to_all | solution.py:51
  112.7 2.6 copy.146
  123.9 21.7 %all-gather.4.cloned.1.call-done = bf16[1024,512]{1,0:T(8,128)(2,1)} async-done(((bf16[256,512]{1,0:T(8,128)(2,1)}), bf16[1024,512]{1,0:T(8,128)(2,1)}) %all-gather.4.cloned.1.call-update) | async-done | bytes 1048592 | tf_op jit(solution)/shard_map/all_gather | solution.py:136
  145.7 4.1 %convolution_convert_fusion.5 = bf16[512,1024]{1,0:T(8,128)(2,1)} fusion(bf16[1024,512]{1,0:T(8,128)(2,1)} %all-gather.4.cloned.1.call-done, bf16[256,1024]{0,1:T(8,128)(2,1)} %get-tuple-element.30, bf16[256,1024]{0,1:T(8,128)(2,1)} %get-tuple-element.31, bf16[256,1024]{0,1:T(8,128)(2,1)} %get-tuple-element.32, bf16[256,1024]{0,1:T(8,128)(2,1)} %get-tuple-element.29), kind=kOutput, calls=%fused_computation.28 | convolution fusion | flops 1082654720 | bytes 4194304 | tf_op jit(solution)/shard_map/dot_general | solution.py:139
  149.8 2.6 broadcast_in_dim_reshape.9
  152.4 2.4 copy.162
  154.8 4.6 %all-to-all-start.2 = ((bf16[1,512,4,256]{3,1,0,2:T(8,128)(2,1)}), bf16[1,512,4,256]{3,1,0,2:T(8,128)(2,1)}, u32[]{:S(2)}, u32[]{:S(2)}) async-start(bf16[1,512,4,256]{3,1,0,2:T(8,128)(2,1)} %copy.162), calls=%async_computation.3 | async-start | bytes 2097152 | tf_op jit(solution)/shard_map/all_to_all | solution.py:142
  159.4 14.9 %all-gather.6.cloned.1.call-done = bf16[1024,512]{1,0:T(8,128)(2,1)} async-done(((bf16[256,512]{1,0:T(8,128)(2,1)}), bf16[1024,512]{1,0:T(8,128)(2,1)}) %all-gather.6.cloned.1.call-update) | async-done | bytes 1048592 | tf_op jit(solution)/shard_map/all_gather | solution.py:136
  174.3 4.1 %convolution_convert_fusion.4 = bf16[512,1024]{1,0:T(8,128)(2,1)} fusion(bf16[1024,512]{1,0:T(8,128)(2,1)} %all-gather.6.cloned.1.call-done, bf16[256,1024]{0,1:T(8,128)(2,1)} %get-tuple-element.30, bf16[256,1024]{0,1:T(8,128)(2,1)} %get-tuple-element.31, bf16[256,1024]{0,1:T(8,128)(2,1)} %get-tuple-element.32, bf16[256,1024]{0,1:T(8,128)(2,1)} %get-tuple-element.29), kind=kOutput, calls=%fused_computation.27 | convolution fusion | flops 1082654720 | bytes 4194304 | tf_op jit(solution)/shard_map/dot_general | solution.py:139
  178.4 2.6 broadcast_in_dim_reshape.10
  181.1 2.3 copy.163
  185.2 4.3 %all-to-all-start.3 = ((bf16[1,512,4,256]{3,1,0,2:T(8,128)(2,1)}), bf16[1,512,4,256]{3,1,0,2:T(8,128)(2,1)}, u32[]{:S(2)}, u32[]{:S(2)}) async-start(bf16[1,512,4,256]{3,1,0,2:T(8,128)(2,1)} %copy.163), calls=%async_computation.4 | async-start | bytes 2097152 | tf_op jit(solution)/shard_map/all_to_all | solution.py:142
  189.5 11.9 %convolution_convert_fusion = bf16[256,4096]{1,0:T(8,128)(2,1)} fusion(bf16[2048,4096]{1,0:T(8,128)(2,1)} %param.10, bf16[32,8,16,128]{3,2,1,0:T(8,128)(2,1)} %bitcast.139), kind=kOutput, calls=%fused_computation | convolution fusion | flops 4296015872 | bytes 19922944 | tf_op jit(solution)/shard_map/dot_general | solution.py:119
  201.5 10.2 %all-gather.8.cloned.1.call-done = bf16[1024,1024]{1,0:T(8,128)(2,1)} async-done(((bf16[256,1024]{1,0:T(8,128)(2,1)}), bf16[1024,1024]{1,0:T(8,128)(2,1)}) %all-gather.8.cloned.1.call-update) | async-done | bytes 2097168 | tf_op jit(solution)/shard_map/all_gather | solution.py:136
  211.7 5.9 %convolution_convert_fusion.2 = bf16[1024,1024]{0,1:T(8,128)(2,1)} fusion(bf16[1024,1024]{1,0:T(8,128)(2,1)} %all-gather.8.cloned.1.call-done, bf16[256,1024]{0,1:T(8,128)(2,1)} %get-tuple-element.30, bf16[256,1024]{0,1:T(8,128)(2,1)} %get-tuple-element.31, bf16[256,1024]{0,1:T(8,128)(2,1)} %get-tuple-element.32, bf16[256,1024]{0,1:T(8,128)(2,1)} %get-tuple-element.29), kind=kOutput, calls=%fused_computation.24 | convolution fusion | flops 2156920832 | bytes 6291456 | tf_op jit(solution)/shard_map/dot_general | solution.py:139
  217.6 4.7 %all-to-all-start.4 = ((bf16[1,1024,4,256]{1,3,0,2:T(8,128)(2,1)}), bf16[1,1024,4,256]{1,3,0,2:T(8,128)(2,1)}, u32[]{:S(2)}, u32[]{:S(2)}) async-start(bf16[1,1024,4,256]{1,3,0,2:T(8,128)(2,1)} %bitcast.145), calls=%async_computation.5 | async-start | bytes 4194304 | tf_op jit(solution)/shard_map/all_to_all | solution.py:142
  222.3 3.0 %slice_multiply_fusion.1 = (f32[1,16,128,128]{3,2,1,0:T(8,128)S(1)}, f32[1,16,128,128]{3,2,1,0:T(8,128)S(1)}) fusion(f32[2,16,128,128]{3,2,1,0:T(8,128)} %get-tuple-element.60, f32[]{:T(128)} %bitcast.23, f32[]{:T(128)} %bitcast.24), kind=kLoop, calls=%fused_computation.39 | loop fusion | flops 524288 | bytes 4194312 | tf_op jit(solution)/shard_map/mul | solution.py:27
  229.2 2.2 fusion.19
  233.7 1.9 copy.161
  239.4 2.1 copy.157
  251.4 19.4 %all-to-all-done.4 = bf16[1,1024,4,256]{1,3,0,2:T(8,128)(2,1)} async-done(((bf16[1,1024,4,256]{1,3,0,2:T(8,128)(2,1)}), bf16[1,1024,4,256]{1,3,0,2:T(8,128)(2,1)}, u32[]{:S(2)}, u32[]{:S(2)}) %all-to-all-start.4) | async-done | bytes 2097184 | tf_op jit(solution)/shard_map/all_to_all | solution.py:142
  270.7 2.1 convert_reduce_fusion
  (107 shorter events, 54.3 us)
Async XLA Ops:
  11.3 5.9 %copy-start.21 = (s32[2]{0:T(128)S(1)}, s32[2]{0:T(128)}, u32[]{:S(2)}) copy-start(s32[2]{0:T(128)} %param.9) | copy-start | bytes 28
  12.7 25.2 %collective-permute-start = (bf16[256,1024]{0,1:T(8,128)(2,1)}, bf16[256,1024]{0,1:T(8,128)(2,1)}, u32[]{:S(2)}, u32[]{:S(2)}) collective-permute-start(bf16[256,1024]{0,1:T(8,128)(2,1)} %bitcast.8), channel_id=1, source_target_pairs={{0,2},{2,0},{4,6},{6,4},{8,10},{10,8},{12,14},{14,12},{16,18},{18,... | collective-permute-start | bytes 1572872 | tf_op jit(solution)/shard_map/ppermute | solution.py:75
  15.7 24.9 %collective-permute-start.1 = (bf16[256,1024]{0,1:T(8,128)(2,1)}, bf16[256,1024]{0,1:T(8,128)(2,1)}, u32[]{:S(2)}, u32[]{:S(2)}) collective-permute-start(bf16[256,1024]{0,1:T(8,128)(2,1)} %bitcast.9), channel_id=1, source_target_pairs={{0,4},{2,6},{4,0},{6,2},{8,12},{10,14},{12,8},{14,10},{16,20},{18,... | collective-permute-start | bytes 1572872 | tf_op jit(solution)/shard_map/ppermute | solution.py:75
  17.2 23.4 %collective-permute-start.2 = (bf16[256,1024]{0,1:T(8,128)(2,1)}, bf16[256,1024]{0,1:T(8,128)(2,1)}, u32[]{:S(2)}, u32[]{:S(2)}) collective-permute-start(bf16[256,1024]{0,1:T(8,128)(2,1)} %bitcast.10), channel_id=1, source_target_pairs={{0,6},{2,4},{4,2},{6,0},{8,14},{10,12},{12,10},{14,8},{16,22},{18,... | collective-permute-start | bytes 1572872 | tf_op jit(solution)/shard_map/ppermute | solution.py:75
  28.7 2.0 copy-start.18
  28.9 2.0 copy-start.2
  30.7 1.2 copy-start.19
  30.7 1.5 copy-start.20
  31.9 1.8 copy-start.5
  78.0 27.5 %all-to-all-start.1 = ((bf16[16,2,128,128]{3,2,1,0:T(8,128)(2,1)}), bf16[16,2,128,128]{3,2,1,0:T(8,128)(2,1)}, u32[]{:S(2)}, u32[]{:S(2)}) async-start(bf16[16,2,128,128]{3,2,1,0:T(8,128)(2,1)} %copy.143), calls=%async_computation.1 | async-start | bytes 2097152 | tf_op jit(solution)/shard_map/all_to_all | solution.py:51
  82.3 63.4 %all-gather.4.cloned.1.call-start = ((), (), s32[]{:S(2)}) async-start(), calls=%async_computation.7 | async-start | bytes 1310720 | tf_op jit(solution)/shard_map/all_gather | solution.py:136
  106.9 1.5 copy-start.10
  106.9 1.9 copy-start.11
  108.8 2.0 copy-start.9
  109.2 1.0 copy-start
  116.8 1.0 copy-start.13
  118.6 55.7 %all-gather.6.cloned.1.call-start = ((), (), s32[]{:S(2)}) async-start(), calls=%async_computation.8 | async-start | bytes 1310720 | tf_op jit(solution)/shard_map/all_gather | solution.py:136
  119.4 92.3 %all-gather.8.cloned.1.call-start = ((), (), s32[]{:S(2)}) async-start(), calls=%async_computation.9 | async-start | bytes 2621440 | tf_op jit(solution)/shard_map/all_gather | solution.py:136
  121.2 1.8 copy-start.14
  154.8 30.4 %all-to-all-start.2 = ((bf16[1,512,4,256]{3,1,0,2:T(8,128)(2,1)}), bf16[1,512,4,256]{3,1,0,2:T(8,128)(2,1)}, u32[]{:S(2)}, u32[]{:S(2)}) async-start(bf16[1,512,4,256]{3,1,0,2:T(8,128)(2,1)} %copy.162), calls=%async_computation.3 | async-start | bytes 2097152 | tf_op jit(solution)/shard_map/all_to_all | solution.py:142
  185.2 32.4 %all-to-all-start.3 = ((bf16[1,512,4,256]{3,1,0,2:T(8,128)(2,1)}), bf16[1,512,4,256]{3,1,0,2:T(8,128)(2,1)}, u32[]{:S(2)}, u32[]{:S(2)}) async-start(bf16[1,512,4,256]{3,1,0,2:T(8,128)(2,1)} %copy.163), calls=%async_computation.4 | async-start | bytes 2097152 | tf_op jit(solution)/shard_map/all_to_all | solution.py:142
  189.5 86.4 %reduce-scatter.2.cloned.1.call-start = ((), (), s32[]{:S(2)}) async-start(), calls=%async_computation.6 | async-start | bytes 3145728 | tf_op jit(solution)/shard_map/reduce_scatter | solution.py:121
  217.6 53.1 %all-to-all-start.4 = ((bf16[1,1024,4,256]{1,3,0,2:T(8,128)(2,1)}), bf16[1,1024,4,256]{1,3,0,2:T(8,128)(2,1)}, u32[]{:S(2)}, u32[]{:S(2)}) async-start(bf16[1,1024,4,256]{1,3,0,2:T(8,128)(2,1)} %bitcast.145), calls=%async_computation.5 | async-start | bytes 4194304 | tf_op jit(solution)/shard_map/all_to_all | solution.py:142
  222.3 3.0 %copy-start.3 = (bf16[32,8,16,128]{3,2,1,0:T(8,128)(2,1)S(1)}, bf16[32,8,16,128]{3,2,1,0:T(8,128)(2,1)}, u32[]{:S(2)}) copy-start(bf16[32,8,16,128]{3,2,1,0:T(8,128)(2,1)} %copy-done.2) | copy-start | bytes 3145732
  225.4 1.2 copy-start.6
  225.4 1.5 copy-start.16
  229.2 2.2 copy-start.12
  235.6 2.0 copy-start.8
  239.4 3.3 %copy-start.1 = (bf16[2,16,128,128]{3,2,1,0:T(8,128)(2,1)S(1)}, bf16[2,16,128,128]{3,2,1,0:T(8,128)(2,1)}, u32[]{:S(2)}) copy-start(bf16[2,16,128,128]{3,2,1,0:T(8,128)(2,1)} %copy-done) | copy-start | bytes 3145732
  239.4 3.3 %copy-start.4 = (bf16[32,8,16,128]{3,2,1,0:T(8,128)(2,1)S(1)}, bf16[32,8,16,128]{3,2,1,0:T(8,128)(2,1)}, u32[]{:S(2)}) copy-start(bf16[32,8,16,128]{3,2,1,0:T(8,128)(2,1)} %copy-done.2) | copy-start | bytes 3145732
  241.5 2.0 copy-start.7
  270.7 2.1 copy-start.17
  (1 other events, 1.0 us)
Sparse Core Ops, SparseCore 0:
  118.8 26.8 all-gather.3
  147.7 26.6 all-gather.5
  176.3 35.2 all-gather.7
Sparse Core Ops, SparseCore 1:
  201.6 9.9 reduce-scatter.1
